TPU v7x, 256 devices: a whole 4x4x8 slice. The times are simulated.
256 devices in a mesh: rows: 16 (over y, x), vocab: 16 (over z, core).
Axes of the slice: x: 4, y: 4, z: 8, core: 2. Of those that a mesh axis runs over, the one named last changes fastest.
Arguments:
- hidden: bfloat16 [16, 1024, 4096], P('rows', None, 'vocab'), may hold values from -1024 to 1024
- mask_positions: int32 [16, 1024], P('rows'), may hold values from 0 to 1023, each once within a row
- counts: int32 [16], replicated, may hold values from 1 to 64, 512 in all
- targets: int32 [16, 1024], P('rows'), may hold values from 0 to 126463
- mask_ratio: int32 [16], P('rows'), may hold values from 1 to 16
- out_weight: bfloat16 [4096, 126464], P(None, ('rows', 'vocab')), may hold values from -1 to 1
Outputs:
- grad_hidden: float32 [16, 1024, 4096], P('rows', None, 'vocab')
Inputs may be any that keep to these rules, and one draw needn't show every extreme that they name: counts sum to 512; some sequence has exactly 64. The first counts[s] entries of row s of mask_positions are its masked positions.
All inputs are finite; a program needn't handle non-finite values.
Results may differ from a plain program's by a relative error of at most 0.0022.
Values may be sent and summed in bfloat16 or wider, within the bound.
No kernel may reach another device: no remote copies, remote signals or barrier semaphores. Data moves between devices by JAX's collectives and lax.ppermute only.
A program may use at most 64 MiB of HBM per device.

v0:
```python
import functools

import jax
import jax.numpy as jnp
from jax import lax
from jax.experimental import pallas as pl
from jax.experimental.pallas import tpu as pltpu
from jax.sharding import Mesh
from jax.sharding import PartitionSpec as P

weight_scale = 4.0
SIDE = 4
DEEP = 8
SEQS = SIDE * SIDE
SLOTS = 32
ROWS = 256
CHUNK = ROWS // 2
AUX = 128
PLANE = ("y", "x")
CHIPS = ("y", "x", "z")
NT = (((1,), (1,)), ((), ()))
TN = (((0,), (0,)), ((), ()))
SENT_SCALE = 4096.0


def chip_index():
    return lax.axis_index("y") * SIDE + lax.axis_index("x")


def first_row(start, core):
    return start + ((start + core) & 1)


def own_rows(counts_ref, ratio_ref, positions_ref, targets_ref, hidden_ref, keep_ref, aux_ref, give_ref, places_ref):
    seq = chip_index()
    core = lax.axis_index("c")
    start = jnp.int32(0)
    count = jnp.int32(0)
    for i in range(SEQS):
        start = start + jnp.where(i < seq, counts_ref[i], 0)
        count = count + jnp.where(i == seq, counts_ref[i], 0)
    length = hidden_ref.shape[0]
    q = lax.broadcasted_iota(jnp.int32, (2 * SLOTS, 1), 0)
    index = jnp.where(q < SLOTS, first_row(start, core), first_row(start, 1 - core)) - start + 2 * (q & (SLOTS - 1))
    valid = index < count
    at = lax.broadcasted_iota(jnp.int32, (2 * SLOTS, 128), 1)
    near = jnp.where(at == index, positions_ref[:, :128].astype(jnp.float32), 0.0)
    places = jnp.where(valid, jnp.sum(near, axis=1, keepdims=True), -1.0)
    places_ref[...] = jnp.transpose(jnp.broadcast_to(places, (2 * SLOTS, 128)))[:8].astype(jnp.int32)
    at = lax.broadcasted_iota(jnp.int32, (2 * SLOTS, length), 1)
    hit = at == places.astype(jnp.int32)
    rows = jnp.dot(jnp.where(hit, 1.0, 0.0).astype(jnp.bfloat16), hidden_ref[...], preferred_element_type=jnp.float32)
    rows = rows.astype(jnp.bfloat16)
    target = jnp.sum(jnp.where(hit, targets_ref[...].astype(jnp.float32), 0.0), axis=1, keepdims=True).astype(jnp.int32)
    lane = lax.broadcasted_iota(jnp.int32, (SLOTS, AUX), 1)
    own = target[:SLOTS]
    digits = jnp.where(lane == 0, own & 127, 0)
    digits = jnp.where(lane == 1, (own >> 7) & 127, digits)
    digits = jnp.where(lane == 2, own >> 14, digits)
    digits = jnp.where(lane == 3, ratio_ref[0], digits)
    keep_ref[...] = rows[:SLOTS]
    aux_ref[...] = digits.astype(jnp.float32).astype(jnp.bfloat16)
    give_ref[...] = rows[SLOTS:]


def slot_dest(counts_ref, slot_index, core):
    slot = slot_index & (SLOTS - 1)
    dest = jnp.full_like(slot_index, -1)
    start = jnp.int32(0)
    for i in range(SEQS):
        end = start + counts_ref[i]
        first = first_row(start, core)
        mine = ((slot_index >> 5) == i) & (first + 2 * slot < end)
        dest = jnp.where(mine, (first >> 1) + slot, dest)
        start = end
    return dest


def pack_rows(counts_ref, slots_ref, low_ref, high_ref, row_ref):
    core = lax.axis_index("c")
    dest = slot_dest(counts_ref, lax.broadcasted_iota(jnp.int32, (1, SEQS * SLOTS), 1), core)
    at = lax.broadcasted_iota(jnp.int32, (ROWS, SEQS * SLOTS), 0)
    pick = jnp.where(at == dest, 1.0, 0.0).astype(jnp.bfloat16)
    packed = jnp.dot(pick, slots_ref[...], preferred_element_type=jnp.float32)
    feat = (slots_ref.shape[1] - AUX) // 2
    own, near = packed[:, :feat], packed[:, feat:2 * feat]
    for at, part in ((0, jnp.where(core == 0, own, near)), (feat, jnp.where(core == 0, near, own))):
        part = part.astype(jnp.bfloat16)
        low_ref[:, at:at + feat] = part[:CHUNK]
        high_ref[:, at:at + feat] = part[CHUNK:]
    digits = jnp.transpose(packed[:, 2 * feat:])
    row_ref[0:1] = digits[0:1] + 128.0 * digits[1:2] + 16384.0 * digits[2:3]
    row_ref[1:2] = weight_scale / digits[3:4]


def features_of(away, span):
    return pl.ds(pl.multiple_of(((lax.axis_index("z") + away) & (DEEP - 1)) * span, span), span)


def add_scores(aways, own_ref, near_ref, chunks, earlier, refs):
    count = own_ref.shape[0]
    for i, away in enumerate(aways):
        block = jnp.concatenate([chunks[2 * i][...], chunks[2 * i + 1][...]], axis=0)
        features = features_of(away, block.shape[1])
        for w_ref, was_ref, ref in zip((own_ref, near_ref), earlier, refs):
            part = lax.dot_general(w_ref[:, features], block, NT, preferred_element_type=jnp.float32)
            if i == 0:
                ref[:count] = part if was_ref is None else was_ref[:count] + part
            else:
                ref[:count] += part


def early_scores(aways, own_ref, near_ref, *refs):
    add_scores(aways, own_ref, near_ref, refs[:-2], (None, None), refs[-2:])


def score_rows(aways, own_ref, near_ref, own_early_ref, near_early_ref, *refs):
    chunks, (own_scores_ref, near_scores_ref, stats_ref) = refs[:-3], refs[-3:]
    count = own_ref.shape[0]
    add_scores(aways, own_ref, near_ref, chunks, (own_early_ref, near_early_ref), (own_scores_ref, near_scores_ref))
    at = lax.broadcasted_iota(jnp.int32, own_scores_ref.shape, 0)
    parts = [jnp.where(at < count, ref[...], -jnp.inf) for ref in (own_scores_ref, near_scores_ref)]
    own_scores_ref[...], near_scores_ref[...] = parts
    top = jnp.maximum(*[jnp.max(part, axis=0, keepdims=True) for part in parts])
    total = sum(jnp.sum(jnp.exp(part - top), axis=0, keepdims=True) for part in parts)
    stats = jnp.concatenate([top, total], axis=0)
    stats_ref[...] = jnp.broadcast_to(stats[None], stats_ref.shape)


def grad_rows(aways, own_slope_ref, near_slope_ref, own_ref, near_ref, *sums_refs):
    count = own_ref.shape[0]
    for i, away in enumerate(aways):
        features = features_of(away, sums_refs[0].shape[1])
        sums = jnp.dot(own_slope_ref[:, :count], own_ref[:, features], preferred_element_type=jnp.float32)
        sums += jnp.dot(near_slope_ref[:, :count], near_ref[:, features], preferred_element_type=jnp.float32)
        sums = sums * SENT_SCALE
        sums_refs[2 * i][...] = sums[:CHUNK]
        sums_refs[2 * i + 1][...] = sums[CHUNK:]


def slope_rows(aways, stats_ref, row_ref, own_scores_ref, near_scores_ref, own_ref, near_ref, own_slope_ref, near_slope_ref, *sums_refs):
    count = own_ref.shape[0]
    tops = stats_ref[:, 0, :]
    top = jnp.max(tops, axis=0, keepdims=True)
    total = jnp.sum(stats_ref[:, 1, :] * jnp.exp(tops - top), axis=0, keepdims=True)
    chip = chip_index() * DEEP + lax.axis_index("z")
    core = lax.axis_index("c")
    target = row_ref[0:1].astype(jnp.int32)
    at = lax.broadcasted_iota(jnp.int32, own_scores_ref.shape, 0)
    for ref, slope, of_core in ((own_scores_ref, own_slope_ref, core), (near_scores_ref, near_slope_ref, 1 - core)):
        local_target = target - (chip * 2 + of_core) * count
        probs = jnp.exp(ref[...] - top) / total
        onehot = jnp.where((at == local_target) & (at < count), 1.0, 0.0)
        slope[...] = jnp.transpose(row_ref[1:2] * (probs - onehot)).astype(jnp.bfloat16)
    grad_rows(aways, own_slope_ref, near_slope_ref, own_ref, near_ref, *sums_refs)


def spread_rows(counts_ref, low_ref, high_ref, slots_ref):
    dest = slot_dest(counts_ref, lax.broadcasted_iota(jnp.int32, (1, SEQS * SLOTS), 1), lax.axis_index("c"))
    at = lax.broadcasted_iota(jnp.int32, (ROWS, SEQS * SLOTS), 0)
    pick = jnp.where(at == dest, 1.0, 0.0).astype(jnp.bfloat16)
    rest = jnp.concatenate([low_ref[...], high_ref[...]], axis=0)
    part = rest.astype(jnp.bfloat16)
    rest = (rest - part.astype(jnp.float32)).astype(jnp.bfloat16)
    slots = lax.dot_general(pick, part, TN, preferred_element_type=jnp.float32)
    slots_ref[...] = slots + lax.dot_general(pick, rest, TN, preferred_element_type=jnp.float32)


def place_rows(places_ref, kept_ref, got_ref, out_ref):
    length = out_ref.shape[0]
    at = lax.broadcasted_iota(jnp.int32, (length, 2 * SLOTS), 0)
    hit = jnp.where(at == places_ref[0:1], 1.0, 0.0).astype(jnp.bfloat16)
    rest = jnp.concatenate([kept_ref[...], got_ref[...]], axis=0)
    out = None
    for _ in range(3):
        part = rest.astype(jnp.bfloat16)
        rest = rest - part.astype(jnp.float32)
        part = jnp.dot(hit, part, preferred_element_type=jnp.float32)
        out = part if out is None else out + part
    out_ref[...] = out


def swap_cores(x):
    return lax.ppermute(x, "c", [(0, 1), (1, 0)])


def pass_on(x, by):
    return lax.ppermute(x, "z", [(i, (i + by) % DEEP) for i in range(DEEP)])


def gather_chips(low, high):
    lows, highs = {0: low}, {0: high}
    for hop in range(1, DEEP // 2 + 1):
        lows[-hop] = pass_on(lows[1 - hop], 1)
        highs[hop] = pass_on(highs[hop - 1], -1)
        if hop < DEEP // 2:
            highs[-hop] = pass_on(highs[1 - hop], 1)
            lows[hop] = pass_on(lows[hop - 1], -1)
    lows[DEEP // 2] = lows[-(DEEP // 2)]
    return [chunk for away in range(DEEP) for chunk in (lows[(away + 3) % DEEP - 3], highs[(away + 3) % DEEP - 3])]


def reduce_chips(lows, highs):
    def send(x, by):
        return pass_on(x, by).astype(jnp.float32)

    def after(x, *others):
        return lax.optimization_barrier((x.astype(jnp.float16), *others))[0]

    half = DEEP // 2
    low_right, high_left = lows[half], highs[half]
    low_left, high_right = lows[half + 1], highs[half - 1]
    for hop in range(1, half):
        right, left = low_right.astype(jnp.float16), high_left.astype(jnp.float16)
        low_left, high_right = after(low_left, right, left), after(high_right, right, left)
        low_right = send(right, 1) + lows[half - hop]
        high_left = send(left, -1) + highs[half + hop]
        low_left, high_right = send(low_left, -1), send(high_right, 1)
        if hop < half - 1:
            low_left = low_left + lows[half + 1 + hop]
            high_right = high_right + highs[half - 1 - hop]
    low = lows[0] + low_left + send(low_right.astype(jnp.float16), 1)
    high = highs[0] + high_right + send(high_left.astype(jnp.float16), -1)
    return low, high


def local(hidden, mask_positions, counts, targets, mask_ratio, own_weight):
    c = lax.axis_index("c")
    features, vocab_dev = own_weight.shape
    wide = -(-vocab_dev // 128) * 128
    length, feat = hidden.shape[1:]
    span = 2 * feat
    smem = pl.BlockSpec(memory_space=pltpu.SMEM)
    vmem = pl.BlockSpec(memory_space=pltpu.VMEM)
    params = pltpu.CompilerParams(vmem_limit_bytes=16 << 20)
    small = pltpu.CompilerParams(vmem_limit_bytes=8 << 20)
    shape = jax.ShapeDtypeStruct

    keep, aux, give, places = pl.pallas_call(
        own_rows,
        out_shape=(
            shape((SLOTS, feat), jnp.bfloat16),
            shape((SLOTS, AUX), jnp.bfloat16),
            shape((SLOTS, feat), jnp.bfloat16),
            shape((8, 2 * SLOTS), jnp.int32),
        ),
        in_specs=[smem, smem, vmem, vmem, vmem],
        out_specs=(vmem,) * 4,
        compiler_params=pltpu.CompilerParams(vmem_limit_bytes=56 << 20),
    )(counts, mask_ratio, mask_positions, targets, hidden[0])
    got = swap_cores(give)

    slots = jnp.concatenate([keep, got, aux], axis=1)
    slots, own_weight = lax.optimization_barrier((slots, own_weight))
    near_t = swap_cores(own_weight).T
    slots = lax.all_to_all(jnp.broadcast_to(slots[None], (SEQS,) + slots.shape), PLANE, 0, 0, tiled=True)
    low, high, row_data = pl.pallas_call(
        pack_rows,
        out_shape=(
            shape((CHUNK, span), jnp.bfloat16),
            shape((CHUNK, span), jnp.bfloat16),
            shape((2, ROWS), jnp.float32),
        ),
        in_specs=[smem, vmem],
        out_specs=(vmem,) * 3,
        compiler_params=small,
    )(counts, slots.reshape(SEQS * SLOTS, span + AUX))

    chunks = gather_chips(low, high)
    pairs = list(zip(chunks[::2], chunks[1::2]))
    own_weight = lax.optimization_barrier((own_weight, pairs[5][0], pairs[3][1]))[0]
    own_t = jnp.where(counts[0] > 0, own_weight, 0).T
    parts = (0, 1, 7, 2, 6), (3, 5, 4)
    score_shapes = (shape((wide, ROWS), jnp.float32),) * 2
    early = pl.pallas_call(
        functools.partial(early_scores, parts[0]),
        out_shape=score_shapes,
        in_specs=[vmem] * (2 + 2 * len(parts[0])),
        out_specs=(vmem,) * 2,
        compiler_params=params,
    )(own_t, near_t, *[chunk for away in parts[0] for chunk in pairs[away]])
    own_scores, near_scores, stats = pl.pallas_call(
        functools.partial(score_rows, parts[1]),
        out_shape=score_shapes + (shape((SEQS * DEEP, 2, ROWS), jnp.float32),),
        in_specs=[vmem] * (4 + 2 * len(parts[1])),
        out_specs=(vmem,) * 3,
        compiler_params=params,
    )(own_t, near_t, *early, *[chunk for away in parts[1] for chunk in pairs[away]])

    stats = lax.all_to_all(stats, CHIPS, 0, 0, tiled=True)
    parts = (4, 5, 3), (6, 2, 7, 1, 0)
    sums_shape = shape((CHUNK, span), jnp.float32)
    slope_shape = shape((ROWS, wide), jnp.bfloat16)
    own_slope, near_slope, *sums = pl.pallas_call(
        functools.partial(slope_rows, parts[0]),
        out_shape=(slope_shape, slope_shape) + (sums_shape,) * (2 * len(parts[0])),
        in_specs=[vmem] * 6,
        out_specs=(vmem,) * (2 + 2 * len(parts[0])),
        compiler_params=params,
    )(stats, row_data, own_scores, near_scores, own_t, near_t)
    more = pl.pallas_call(
        functools.partial(grad_rows, parts[1]),
        out_shape=(sums_shape,) * (2 * len(parts[1])),
        in_specs=[vmem] * 4,
        out_specs=(vmem,) * (2 * len(parts[1])),
        compiler_params=params,
    )(own_slope, near_slope, own_t, near_t)
    sums = lax.optimization_barrier((*sums, *more))
    lows = dict(zip(parts[0] + parts[1], sums[::2]))
    highs = dict(zip(parts[0] + parts[1], sums[1::2]))

    low, high = reduce_chips(lows, highs)
    back = pl.pallas_call(
        spread_rows,
        out_shape=shape((SEQS * SLOTS, span), jnp.float32),
        in_specs=[smem, vmem, vmem],
        out_specs=vmem,
        compiler_params=small,
    )(counts, low, high)
    back = back.astype(jnp.float16).reshape(SEQS, SLOTS, span)
    first_core = c == 0
    back = lax.all_to_all(back, PLANE, 0, 0, tiled=True)
    back = jnp.sum(back.astype(jnp.float32), axis=0) * (1.0 / SENT_SCALE)
    kept = jnp.where(first_core, back[:, :feat], back[:, feat:])
    given = jnp.where(first_core, back[:, feat:], back[:, :feat])
    grad = pl.pallas_call(
        place_rows,
        out_shape=shape((length, feat), jnp.float32),
        in_specs=[vmem] * 3,
        out_specs=vmem,
        compiler_params=small,
    )(places, kept, swap_cores(given))
    return grad[None]


def solution(mesh):
    fine = Mesh(mesh.devices.reshape(SIDE, SIDE, DEEP, 2), CHIPS + ("c",))
    vocab = ("z", "c")
    return jax.shard_map(
        local,
        mesh=fine,
        in_specs=(
            P(PLANE, None, vocab),
            P(PLANE, None),
            P(),
            P(PLANE, None),
            P(PLANE),
            P(None, CHIPS + ("c",)),
        ),
        out_specs=P(PLANE, None, vocab),
        check_vma=False,
    )
```

profile of v0, /device:TPU:1, one launch (start us, length us, event | category | flops | bytes accessed | tf_op | source)
XLA Modules:
  0.0 133.9 jit_solution(11216463179196422738)
XLA Ops:
  0.7 2.0 %shard_map.64 = (bf16[32,256]{1,0:T(8,128)(2,1)}, bf16[32,128]{1,0:T(8,128)(2,1)}, bf16[32,256]{1,0:T(8,128)(2,1)}, s32[8,64]{1,0:T(8,128)}) custom-call(s32[16]{0:T(128)} %counts_ref.5, s32[1]{0:T(128)S(6)} %copy.7.ratio_ref, s32[1,1024]{1,0:T(1,128)} %positions_ref.1, s32[1,1024]{1,0:T(1,128)} %targets_ref.1, bf16[1024,256]{1,0:T(8,128)(2,1)} %bitcast.15), custom_call_target="tpu_custom_call" | custom-call | tf_op jit(solution)/shard_map/pallas_call | solution.py:239
  2.6 3.2 %collective-permute-start = (bf16[32,256]{1,0:T(8,128)(2,1)}, bf16[32,256]{1,0:T(8,128)(2,1)S(1)}, u32[]{:S(2)}, u32[]{:S(2)}) collective-permute-start(bf16[32,256]{1,0:T(8,128)(2,1)} %get-tuple-element.62), channel_id=1, source_target_pairs={{0,1},{1,0},{2,3},{3,2},{4,5},{5,4},{6,7},{7,6},{8,9},{9,8},{10,11... | collective-permute-start | bytes 49160 | tf_op jit(solution)/shard_map/ppermute | solution.py:184
  5.9 1.0 collective-permute-done
  6.9 0.7 pad_maximum_fusion
  7.7 0.3 collective-permute-start.7
  8.0 0.1 broadcast_in_dim.13
  8.1 17.4 %all_to_all.15 = bf16[16,32,640]{2,1,0:T(8,128)(2,1)S(1)} all-to-all(bf16[16,32,640]{2,1,0:T(8,128)(2,1)S(1)} %broadcast_in_dim.13), channel_id=1, replica_groups=mesh['y'=4,'x'=4,'z'=8,'c'=2] {'y','x'}, dimensions={0} | all-to-all | bytes 1310720 | tf_op jit(solution)/shard_map/all_to_all | solution.py:256
  25.5 0.7 copy-done
  26.1 1.0 shard_map.65
  27.1 1.7 %collective-permute-start.1 = (bf16[128,512]{1,0:T(8,128)(2,1)S(1)}, bf16[128,512]{1,0:T(8,128)(2,1)S(1)}, u32[]{:S(2)}, u32[]{:S(2)}) collective-permute-start(bf16[128,512]{1,0:T(8,128)(2,1)S(1)} %get-tuple-element.66.refs_0_), channel_id=1, source_target_pairs={{0,2},{2,4},{4,6},{6,8},{8,10},{10,12},{12,14},{14,0},{1,3},{3,5},... | collective-permute-start | bytes 393224 | tf_op jit(solution)/shard_map/ppermute | solution.py:188
  28.8 4.0 %collective-permute-start.4 = (bf16[128,512]{1,0:T(8,128)(2,1)S(1)}, bf16[128,512]{1,0:T(8,128)(2,1)S(1)}, u32[]{:S(2)}, u32[]{:S(2)}) collective-permute-start(bf16[128,512]{1,0:T(8,128)(2,1)S(1)} %get-tuple-element.67.refs_1_), channel_id=1, source_target_pairs={{0,14},{2,0},{4,2},{6,4},{8,6},{10,8},{12,10},{14,12},{1,15},{3,1}... | collective-permute-start | bytes 393224 | tf_op jit(solution)/shard_map/ppermute | solution.py:188
  32.9 1.4 %collective-permute-start.8 = (bf16[128,512]{1,0:T(8,128)(2,1)S(1)}, bf16[128,512]{1,0:T(8,128)(2,1)S(1)}, u32[]{:S(2)}, u32[]{:S(2)}) collective-permute-start(bf16[128,512]{1,0:T(8,128)(2,1)S(1)} %get-tuple-element.66.refs_0_), channel_id=1, source_target_pairs={{0,14},{2,0},{4,2},{6,4},{8,6},{10,8},{12,10},{14,12},{1,15},{3,1}... | collective-permute-start | bytes 393224 | tf_op jit(solution)/shard_map/ppermute | solution.py:188
  34.2 0.1 collective-permute-start.9
  34.3 0.8 collective-permute-done.1.refs_4_
  35.1 2.8 %collective-permute-start.5 = (bf16[128,512]{1,0:T(8,128)(2,1)S(1)}, bf16[128,512]{1,0:T(8,128)(2,1)S(1)}, u32[]{:S(2)}, u32[]{:S(2)}) collective-permute-start(bf16[128,512]{1,0:T(8,128)(2,1)S(1)} %collective-permute-done.4.refs_3_), channel_id=1, source_target_pairs={{0,14},{2,0},{4,2},{6,4},{8,6},{10,8},{12,10},{14,12},{1,15},{3,1}... | collective-permute-start | bytes 393224 | tf_op jit(solution)/shard_map/ppermute | solution.py:188
  37.9 0.0 collective-permute-done.8.refs_2_
  37.9 2.7 %collective-permute-start.10 = (bf16[128,512]{1,0:T(8,128)(2,1)S(1)}, bf16[128,512]{1,0:T(8,128)(2,1)S(1)}, u32[]{:S(2)}, u32[]{:S(2)}) collective-permute-start(bf16[128,512]{1,0:T(8,128)(2,1)S(1)} %collective-permute-done.8.refs_2_), channel_id=1, source_target_pairs={{0,14},{2,0},{4,2},{6,4},{8,6},{10,8},{12,10},{14,12},{1,15},{3,1}... | collective-permute-start | bytes 393224 | tf_op jit(solution)/shard_map/ppermute | solution.py:188
  40.6 0.0 collective-permute-start.11
  40.6 0.5 collective-permute-done.2.refs_8_
  41.1 0.0 collective-permute-start.3
  41.1 2.7 %collective-permute-start.6 = (bf16[128,512]{1,0:T(8,128)(2,1)S(1)}, bf16[128,512]{1,0:T(8,128)(2,1)S(1)}, u32[]{:S(2)}, u32[]{:S(2)}) collective-permute-start(bf16[128,512]{1,0:T(8,128)(2,1)S(1)} %collective-permute-done.5.refs_7_), channel_id=1, source_target_pairs={{0,14},{2,0},{4,2},{6,4},{8,6},{10,8},{12,10},{14,12},{1,15},{3,1}... | collective-permute-start | bytes 393224 | tf_op jit(solution)/shard_map/ppermute | solution.py:188
  44.5 0.0 collective-permute-done.10.refs_6_
  44.5 1.5 %collective-permute-start.12 = (bf16[128,512]{1,0:T(8,128)(2,1)S(1)}, bf16[128,512]{1,0:T(8,128)(2,1)S(1)}, u32[]{:S(2)}, u32[]{:S(2)}) collective-permute-start(bf16[128,512]{1,0:T(8,128)(2,1)S(1)} %collective-permute-done.10.refs_6_), channel_id=1, source_target_pairs={{0,14},{2,0},{4,2},{6,4},{8,6},{10,8},{12,10},{14,12},{1,15},{3,1}... | collective-permute-start | bytes 393224 | tf_op jit(solution)/shard_map/ppermute | solution.py:188
  46.0 1.0 collective-permute-done.3.refs_2_
  47.0 0.1 collective-permute-done.6.refs_1_
  47.1 0.6 collective-permute-start.14
  47.7 2.7 %collective-permute-start.15 = (bf16[128,512]{1,0:T(8,128)(2,1)S(1)}, bf16[128,512]{1,0:T(8,128)(2,1)S(1)}, u32[]{:S(2)}, u32[]{:S(2)}) collective-permute-start(bf16[128,512]{1,0:T(8,128)(2,1)S(1)} %collective-permute-done.6.refs_1_), channel_id=1, source_target_pairs={{0,14},{2,0},{4,2},{6,4},{8,6},{10,8},{12,10},{14,12},{1,15},{3,1}... | collective-permute-start | bytes 393224 | tf_op jit(solution)/shard_map/ppermute | solution.py:188
  50.5 2.4 %select_bitcast_fusion.own_ref = bf16[494,4096]{1,0:T(8,128)(2,1)S(1)} fusion(bf16[4096,494]{0,1:T(8,128)(2,1)} %param.11, pred[]{:T(512)} %bitcast.1), kind=kLoop, calls=%fused_computation | loop fusion | flops 2023424 | bytes 8093697 | tf_op jit(solution)/shard_map/transpose | solution.py:272
  52.9 0.0 collective-permute-done.7
  52.9 1.5 %shard_map.66 = (f32[512,256]{1,0:T(8,128)S(1)}, f32[512,256]{1,0:T(8,128)S(1)}) custom-call(bf16[494,4096]{1,0:T(8,128)(2,1)S(1)} %select_bitcast_fusion.own_ref, bf16[494,4096]{1,0:T(8,128)(2,1)S(1)} %bitcast.9, bf16[128,512]{1,0:T(8,128)(2,1)S(1)} %get-tuple-element.66.refs_0_, bf16[128,512]{1,0:T(8,128)(2,1)S(1)} %get-tuple-element.67.refs_1_, ...), custom_call_target="tpu_custom_call" | custom-call | tf_op jit(solution)/shard_map/pallas_call | solution.py:275
  54.4 0.0 collective-permute-done.12.refs_0_
  54.4 0.0 collective-permute-done.13.refs_3_
  54.5 0.0 collective-permute-done.15.refs_5_
  54.5 1.2 shard_map.67
  55.7 21.0 %all_to_all.16.stats_ref = f32[128,2,256]{2,1,0:T(2,128)S(1)} all-to-all(f32[128,2,256]{2,1,0:T(2,128)S(1)} %get-tuple-element.71), channel_id=1, replica_groups=mesh['y'=4,'x'=4,'z'=8,'c'=2] {'y','x','z'}, dimensions={0} | all-to-all | bytes 524288 | tf_op jit(solution)/shard_map/all_to_all | solution.py:290
  76.7 1.4 %shard_map.68 = (bf16[256,512]{1,0:T(8,128)(2,1)S(1)}, bf16[256,512]{1,0:T(8,128)(2,1)S(1)}, f32[128,512]{1,0:T(8,128)S(1)}, f32[128,512]{1,0:T(8,128)S(1)}, f32...) custom-call(f32[128,2,256]{2,1,0:T(2,128)S(1)} %all_to_all.16.stats_ref, ...), custom_call_target="tpu_custom_call" | custom-call | tf_op jit(solution)/shard_map/pallas_call | solution.py:294
  78.1 1.5 %shard_map.69 = (f32[128,512]{1,0:T(8,128)S(1)}, f32[128,512]{1,0:T(8,128)S(1)}, f32[128,512]{1,0:T(8,128)S(1)}, f32[128,512]{1,0:T(8,128)S(1)}, f32[128,512]{1,...) custom-call(bf16[256,512]{1,0:T(8,128)(2,1)S(1)} %get-tuple-element., ...), custom_call_target="tpu_custom_call" | custom-call | tf_op jit(solution)/shard_map/pallas_call | solution.py:301
  79.7 0.0 copy-start.1
  79.7 0.4 collective-permute-start.17
  80.1 2.4 %collective-permute-start.18 = (f16[128,512]{1,0:T(8,128)(2,1)S(1)}, f16[128,512]{1,0:T(8,128)(2,1)S(1)}, u32[]{:S(2)}, u32[]{:S(2)}) collective-permute-start(f16[128,512]{1,0:T(8,128)(2,1)S(1)} %convert_element_type.94), channel_id=1, source_target_pairs={{0,14},{2,0},{4,2},{6,4},{8,6},{10,8},{12,10},{14,12},{1,15},{3,1}... | collective-permute-start | bytes 393224 | tf_op jit(solution)/shard_map/ppermute | solution.py:188
  82.6 0.0 collective-permute-start.25
  82.6 2.7 %collective-permute-start.16 = (f16[128,512]{1,0:T(8,128)(2,1)S(1)}, f16[128,512]{1,0:T(8,128)(2,1)S(1)}, u32[]{:S(2)}, u32[]{:S(2)}) collective-permute-start(f16[128,512]{1,0:T(8,128)(2,1)S(1)} %convert_element_type.92), channel_id=1, source_target_pairs={{0,14},{2,0},{4,2},{6,4},{8,6},{10,8},{12,10},{14,12},{1,15},{3,1}... | collective-permute-start | bytes 393224 | tf_op jit(solution)/shard_map/ppermute | solution.py:188
  85.4 0.1 collective-permute-start.20
  85.6 2.7 %collective-permute-start.21 = (f16[128,512]{1,0:T(8,128)(2,1)S(1)}, f16[128,512]{1,0:T(8,128)(2,1)S(1)}, u32[]{:S(2)}, u32[]{:S(2)}) collective-permute-start(f16[128,512]{1,0:T(8,128)(2,1)S(1)} %add_convert_fusion.7), channel_id=1, source_target_pairs={{0,14},{2,0},{4,2},{6,4},{8,6},{10,8},{12,10},{14,12},{1,15},{3,1}... | collective-permute-start | bytes 393224 | tf_op jit(solution)/shard_map/ppermute | solution.py:188
  88.3 0.3 collective-permute-start.26
  88.7 2.7 %collective-permute-start.19 = (f16[128,512]{1,0:T(8,128)(2,1)S(1)}, f16[128,512]{1,0:T(8,128)(2,1)S(1)}, u32[]{:S(2)}, u32[]{:S(2)}) collective-permute-start(f16[128,512]{1,0:T(8,128)(2,1)S(1)} %add_convert_fusion.9), channel_id=1, source_target_pairs={{0,14},{2,0},{4,2},{6,4},{8,6},{10,8},{12,10},{14,12},{1,15},{3,1}... | collective-permute-start | bytes 393224 | tf_op jit(solution)/shard_map/ppermute | solution.py:188
  91.5 0.1 collective-permute-start.23
  91.6 2.7 %collective-permute-start.28 = (f16[128,512]{1,0:T(8,128)(2,1)S(1)}, f16[128,512]{1,0:T(8,128)(2,1)S(1)}, u32[]{:S(2)}, u32[]{:S(2)}) collective-permute-start(f16[128,512]{1,0:T(8,128)(2,1)S(1)} %add_convert_fusion.4), channel_id=1, source_target_pairs={{0,14},{2,0},{4,2},{6,4},{8,6},{10,8},{12,10},{14,12},{1,15},{3,1}... | collective-permute-start | bytes 393224 | tf_op jit(solution)/shard_map/ppermute | solution.py:188
  94.4 0.1 add_convert_fusion.1
  94.5 2.5 %collective-permute-start.22 = (f16[128,512]{1,0:T(8,128)(2,1)S(1)}, f16[128,512]{1,0:T(8,128)(2,1)S(1)}, u32[]{:S(2)}, u32[]{:S(2)}) collective-permute-start(f16[128,512]{1,0:T(8,128)(2,1)S(1)} %get-tuple-element.105), channel_id=1, source_target_pairs={{0,14},{2,0},{4,2},{6,4},{8,6},{10,8},{12,10},{14,12},{1,15},{3,1}... | collective-permute-start | bytes 393224 | tf_op jit(solution)/shard_map/ppermute | solution.py:188
  97.0 0.1 collective-permute-done.23
  97.1 0.1 collective-permute-start.24
  97.3 3.0 %collective-permute-start.29 = (f16[128,512]{1,0:T(8,128)(2,1)S(1)}, f16[128,512]{1,0:T(8,128)(2,1)S(1)}, u32[]{:S(2)}, u32[]{:S(2)}) collective-permute-start(f16[128,512]{1,0:T(8,128)(2,1)S(1)} %add_convert_fusion), channel_id=1, source_target_pairs={{0,14},{2,0},{4,2},{6,4},{8,6},{10,8},{12,10},{14,12},{1,15},{3,1}... | collective-permute-start | bytes 393224 | tf_op jit(solution)/shard_map/ppermute | solution.py:188
  100.3 4.6 %collective-permute-done.24 = f16[128,512]{1,0:T(8,128)(2,1)S(1)} collective-permute-done((f16[128,512]{1,0:T(8,128)(2,1)S(1)}, f16[128,512]{1,0:T(8,128)(2,1)S(1)}, u32[]{:S(2)}, u32[]{:S(2)}) %collective-permute-start.24) | collective-permute-done | bytes 131104 | tf_op jit(solution)/shard_map/ppermute | solution.py:188
  104.8 0.1 convert_add_fusion.1.low_ref
  104.9 0.1 convert_add_fusion.high_ref
  105.0 1.1 shard_map.70
  106.1 0.9 convert_element_type.120
  107.0 3.6 %all-to-all-start.2 = ((f16[16,32,512]{2,1,0:T(8,128)(2,1)}), f16[16,32,512]{2,1,0:T(8,128)(2,1)S(1)}, u32[]{:S(2)}, u32[]{:S(2)}) async-start(f16[16,32,512]{2,1,0:T(8,128)(2,1)} %bitcast.5), calls=%async_computation.2 | async-start | bytes 1048576 | tf_op jit(solution)/shard_map/all_to_all | solution.py:322
  110.6 8.9 %all-to-all-done.2 = f16[16,32,512]{2,1,0:T(8,128)(2,1)S(1)} async-done(((f16[16,32,512]{2,1,0:T(8,128)(2,1)}), f16[16,32,512]{2,1,0:T(8,128)(2,1)S(1)}, u32[]{:S(2)}, u32[]{:S(2)}) %all-to-all-start.2) | async-done | bytes 524320 | tf_op jit(solution)/shard_map/all_to_all | solution.py:322
  119.5 0.1 convert_reduce_fusion
  119.6 11.8 %collective-permute-start.30 = (f32[32,256]{1,0:T(8,128)S(1)}, f32[32,256]{1,0:T(8,128)S(1)}, u32[]{:S(2)}, u32[]{:S(2)}) collective-permute-start(f32[32,256]{1,0:T(8,128)S(1)} %get-tuple-element.115), channel_id=1, source_target_pairs={{0,1},{1,0},{2,3},{3,2},{4,5},{5,4},{6,7},{7,6},{8,9},{9,8},{10,11... | collective-permute-start | bytes 98312 | tf_op jit(solution)/shard_map/ppermute | solution.py:184
  131.5 0.9 collective-permute-done.30.got_ref
  132.3 1.5 %shard_map.71 = f32[1024,256]{1,0:T(8,128)} custom-call(s32[8,64]{1,0:T(8,128)S(1)} %copy-done.2, f32[32,256]{1,0:T(8,128)S(1)} %get-tuple-element.116.kept_ref, f32[32,256]{1,0:T(8,128)S(1)} %collective-permute-done.30.got_ref), custom_call_target="tpu_custom_call" | custom-call | tf_op jit(solution)/shard_map/pallas_call | solution.py:326
  (38 shorter events, 0.5 us)
Async XLA Ops:
  2.6 4.3 %collective-permute-start = (bf16[32,256]{1,0:T(8,128)(2,1)}, bf16[32,256]{1,0:T(8,128)(2,1)S(1)}, u32[]{:S(2)}, u32[]{:S(2)}) collective-permute-start(bf16[32,256]{1,0:T(8,128)(2,1)} %get-tuple-element.62), channel_id=1, source_target_pairs={{0,1},{1,0},{2,3},{3,2},{4,5},{5,4},{6,7},{7,6},{8,9},{9,8},{10,11... | collective-permute-start | bytes 49160 | tf_op jit(solution)/shard_map/ppermute | solution.py:184
  7.7 45.2 %collective-permute-start.7 = (bf16[4096,494]{0,1:T(8,128)(2,1)}, bf16[4096,494]{0,1:T(8,128)(2,1)S(1)}, u32[]{:S(2)}, u32[]{:S(2)}) collective-permute-start(bf16[4096,494]{0,1:T(8,128)(2,1)} %param.11), channel_id=1, source_target_pairs={{0,1},{1,0},{2,3},{3,2},{4,5},{5,4},{6,7},{7,6},{8,9},{9,8},{10,11... | collective-permute-start | bytes 12140552 | tf_op jit(solution)/shard_map/ppermute | solution.py:184
  25.5 0.7 copy-start
  27.1 8.0 %collective-permute-start.1 = (bf16[128,512]{1,0:T(8,128)(2,1)S(1)}, bf16[128,512]{1,0:T(8,128)(2,1)S(1)}, u32[]{:S(2)}, u32[]{:S(2)}) collective-permute-start(bf16[128,512]{1,0:T(8,128)(2,1)S(1)} %get-tuple-element.66.refs_0_), channel_id=1, source_target_pairs={{0,2},{2,4},{4,6},{6,8},{8,10},{10,12},{12,14},{14,0},{1,3},{3,5},... | collective-permute-start | bytes 393224 | tf_op jit(solution)/shard_map/ppermute | solution.py:188
  28.8 6.3 %collective-permute-start.4 = (bf16[128,512]{1,0:T(8,128)(2,1)S(1)}, bf16[128,512]{1,0:T(8,128)(2,1)S(1)}, u32[]{:S(2)}, u32[]{:S(2)}) collective-permute-start(bf16[128,512]{1,0:T(8,128)(2,1)S(1)} %get-tuple-element.67.refs_1_), channel_id=1, source_target_pairs={{0,14},{2,0},{4,2},{6,4},{8,6},{10,8},{12,10},{14,12},{1,15},{3,1}... | collective-permute-start | bytes 393224 | tf_op jit(solution)/shard_map/ppermute | solution.py:188
  32.9 5.0 %collective-permute-start.8 = (bf16[128,512]{1,0:T(8,128)(2,1)S(1)}, bf16[128,512]{1,0:T(8,128)(2,1)S(1)}, u32[]{:S(2)}, u32[]{:S(2)}) collective-permute-start(bf16[128,512]{1,0:T(8,128)(2,1)S(1)} %get-tuple-element.66.refs_0_), channel_id=1, source_target_pairs={{0,14},{2,0},{4,2},{6,4},{8,6},{10,8},{12,10},{14,12},{1,15},{3,1}... | collective-permute-start | bytes 393224 | tf_op jit(solution)/shard_map/ppermute | solution.py:188
  34.2 6.3 %collective-permute-start.9 = (bf16[128,512]{1,0:T(8,128)(2,1)S(1)}, bf16[128,512]{1,0:T(8,128)(2,1)S(1)}, u32[]{:S(2)}, u32[]{:S(2)}) collective-permute-start(bf16[128,512]{1,0:T(8,128)(2,1)S(1)} %get-tuple-element.67.refs_1_), channel_id=1, source_target_pairs={{0,2},{2,4},{4,6},{6,8},{8,10},{10,12},{12,14},{14,0},{1,3},{3,5},... | collective-permute-start | bytes 393224 | tf_op jit(solution)/shard_map/ppermute | solution.py:188
  35.1 6.0 %collective-permute-start.2 = (bf16[128,512]{1,0:T(8,128)(2,1)S(1)}, bf16[128,512]{1,0:T(8,128)(2,1)S(1)}, u32[]{:S(2)}, u32[]{:S(2)}) collective-permute-start(bf16[128,512]{1,0:T(8,128)(2,1)S(1)} %collective-permute-done.1.refs_4_), channel_id=1, source_target_pairs={{0,2},{2,4},{4,6},{6,8},{8,10},{10,12},{12,14},{14,0},{1,3},{3,5},... | collective-permute-start | bytes 393224 | tf_op jit(solution)/shard_map/ppermute | solution.py:188
  35.1 6.0 %collective-permute-start.5 = (bf16[128,512]{1,0:T(8,128)(2,1)S(1)}, bf16[128,512]{1,0:T(8,128)(2,1)S(1)}, u32[]{:S(2)}, u32[]{:S(2)}) collective-permute-start(bf16[128,512]{1,0:T(8,128)(2,1)S(1)} %collective-permute-done.4.refs_3_), channel_id=1, source_target_pairs={{0,14},{2,0},{4,2},{6,4},{8,6},{10,8},{12,10},{14,12},{1,15},{3,1}... | collective-permute-start | bytes 393224 | tf_op jit(solution)/shard_map/ppermute | solution.py:188
  37.9 6.6 %collective-permute-start.10 = (bf16[128,512]{1,0:T(8,128)(2,1)S(1)}, bf16[128,512]{1,0:T(8,128)(2,1)S(1)}, u32[]{:S(2)}, u32[]{:S(2)}) collective-permute-start(bf16[128,512]{1,0:T(8,128)(2,1)S(1)} %collective-permute-done.8.refs_2_), channel_id=1, source_target_pairs={{0,14},{2,0},{4,2},{6,4},{8,6},{10,8},{12,10},{14,12},{1,15},{3,1}... | collective-permute-start | bytes 393224 | tf_op jit(solution)/shard_map/ppermute | solution.py:188
  40.6 5.4 %collective-permute-start.11 = (bf16[128,512]{1,0:T(8,128)(2,1)S(1)}, bf16[128,512]{1,0:T(8,128)(2,1)S(1)}, u32[]{:S(2)}, u32[]{:S(2)}) collective-permute-start(bf16[128,512]{1,0:T(8,128)(2,1)S(1)} %collective-permute-done.9.refs_5_), channel_id=1, source_target_pairs={{0,2},{2,4},{4,6},{6,8},{8,10},{10,12},{12,14},{14,0},{1,3},{3,5},... | collective-permute-start | bytes 393224 | tf_op jit(solution)/shard_map/ppermute | solution.py:188
  41.1 5.9 %collective-permute-start.3 = (bf16[128,512]{1,0:T(8,128)(2,1)S(1)}, bf16[128,512]{1,0:T(8,128)(2,1)S(1)}, u32[]{:S(2)}, u32[]{:S(2)}) collective-permute-start(bf16[128,512]{1,0:T(8,128)(2,1)S(1)} %collective-permute-done.2.refs_8_), channel_id=1, source_target_pairs={{0,2},{2,4},{4,6},{6,8},{8,10},{10,12},{12,14},{14,0},{1,3},{3,5},... | collective-permute-start | bytes 393224 | tf_op jit(solution)/shard_map/ppermute | solution.py:188
  41.1 6.0 %collective-permute-start.6 = (bf16[128,512]{1,0:T(8,128)(2,1)S(1)}, bf16[128,512]{1,0:T(8,128)(2,1)S(1)}, u32[]{:S(2)}, u32[]{:S(2)}) collective-permute-start(bf16[128,512]{1,0:T(8,128)(2,1)S(1)} %collective-permute-done.5.refs_7_), channel_id=1, source_target_pairs={{0,14},{2,0},{4,2},{6,4},{8,6},{10,8},{12,10},{14,12},{1,15},{3,1}... | collective-permute-start | bytes 393224 | tf_op jit(solution)/shard_map/ppermute | solution.py:188
  44.5 10.0 %collective-permute-start.12 = (bf16[128,512]{1,0:T(8,128)(2,1)S(1)}, bf16[128,512]{1,0:T(8,128)(2,1)S(1)}, u32[]{:S(2)}, u32[]{:S(2)}) collective-permute-start(bf16[128,512]{1,0:T(8,128)(2,1)S(1)} %collective-permute-done.10.refs_6_), channel_id=1, source_target_pairs={{0,14},{2,0},{4,2},{6,4},{8,6},{10,8},{12,10},{14,12},{1,15},{3,1}... | collective-permute-start | bytes 393224 | tf_op jit(solution)/shard_map/ppermute | solution.py:188
  46.0 8.4 %collective-permute-start.13 = (bf16[128,512]{1,0:T(8,128)(2,1)S(1)}, bf16[128,512]{1,0:T(8,128)(2,1)S(1)}, u32[]{:S(2)}, u32[]{:S(2)}) collective-permute-start(bf16[128,512]{1,0:T(8,128)(2,1)S(1)} %collective-permute-done.11.refs_9_), channel_id=1, source_target_pairs={{0,2},{2,4},{4,6},{6,8},{8,10},{10,12},{12,14},{14,0},{1,3},{3,5},... | collective-permute-start | bytes 393224 | tf_op jit(solution)/shard_map/ppermute | solution.py:188
  47.1 7.3 %collective-permute-start.14 = (bf16[128,512]{1,0:T(8,128)(2,1)S(1)}, bf16[128,512]{1,0:T(8,128)(2,1)S(1)}, u32[]{:S(2)}, u32[]{:S(2)}) collective-permute-start(bf16[128,512]{1,0:T(8,128)(2,1)S(1)} %collective-permute-done.3.refs_2_), channel_id=1, source_target_pairs={{0,2},{2,4},{4,6},{6,8},{8,10},{10,12},{12,14},{14,0},{1,3},{3,5},... | collective-permute-start | bytes 393224 | tf_op jit(solution)/shard_map/ppermute | solution.py:188
  47.7 6.7 %collective-permute-start.15 = (bf16[128,512]{1,0:T(8,128)(2,1)S(1)}, bf16[128,512]{1,0:T(8,128)(2,1)S(1)}, u32[]{:S(2)}, u32[]{:S(2)}) collective-permute-start(bf16[128,512]{1,0:T(8,128)(2,1)S(1)} %collective-permute-done.6.refs_1_), channel_id=1, source_target_pairs={{0,14},{2,0},{4,2},{6,4},{8,6},{10,8},{12,10},{14,12},{1,15},{3,1}... | collective-permute-start | bytes 393224 | tf_op jit(solution)/shard_map/ppermute | solution.py:188
  79.7 25.3 %copy-start.1 = (s32[16]{0:T(128)S(1)}, s32[16]{0:T(128)}, u32[]{:S(2)}) copy-start(s32[16]{0:T(128)} %counts_ref.5) | copy-start | bytes 196
  79.7 5.7 %collective-permute-start.17 = (f16[128,512]{1,0:T(8,128)(2,1)S(1)}, f16[128,512]{1,0:T(8,128)(2,1)S(1)}, u32[]{:S(2)}, u32[]{:S(2)}) collective-permute-start(f16[128,512]{1,0:T(8,128)(2,1)S(1)} %convert_element_type.93), channel_id=1, source_target_pairs={{0,2},{2,4},{4,6},{6,8},{8,10},{10,12},{12,14},{14,0},{1,3},{3,5},... | collective-permute-start | bytes 393224 | tf_op jit(solution)/shard_map/ppermute | solution.py:188
  80.1 5.4 %collective-permute-start.18 = (f16[128,512]{1,0:T(8,128)(2,1)S(1)}, f16[128,512]{1,0:T(8,128)(2,1)S(1)}, u32[]{:S(2)}, u32[]{:S(2)}) collective-permute-start(f16[128,512]{1,0:T(8,128)(2,1)S(1)} %convert_element_type.94), channel_id=1, source_target_pairs={{0,14},{2,0},{4,2},{6,4},{8,6},{10,8},{12,10},{14,12},{1,15},{3,1}... | collective-permute-start | bytes 393224 | tf_op jit(solution)/shard_map/ppermute | solution.py:188
  82.6 5.7 %collective-permute-start.25 = (f16[128,512]{1,0:T(8,128)(2,1)S(1)}, f16[128,512]{1,0:T(8,128)(2,1)S(1)}, u32[]{:S(2)}, u32[]{:S(2)}) collective-permute-start(f16[128,512]{1,0:T(8,128)(2,1)S(1)} %convert_element_type.111), channel_id=1, source_target_pairs={{0,2},{2,4},{4,6},{6,8},{8,10},{10,12},{12,14},{14,0},{1,3},{3,5},... | collective-permute-start | bytes 393224 | tf_op jit(solution)/shard_map/ppermute | solution.py:188
  82.6 6.1 %collective-permute-start.16 = (f16[128,512]{1,0:T(8,128)(2,1)S(1)}, f16[128,512]{1,0:T(8,128)(2,1)S(1)}, u32[]{:S(2)}, u32[]{:S(2)}) collective-permute-start(f16[128,512]{1,0:T(8,128)(2,1)S(1)} %convert_element_type.92), channel_id=1, source_target_pairs={{0,14},{2,0},{4,2},{6,4},{8,6},{10,8},{12,10},{14,12},{1,15},{3,1}... | collective-permute-start | bytes 393224 | tf_op jit(solution)/shard_map/ppermute | solution.py:188
  85.4 6.0 %collective-permute-start.20 = (f16[128,512]{1,0:T(8,128)(2,1)S(1)}, f16[128,512]{1,0:T(8,128)(2,1)S(1)}, u32[]{:S(2)}, u32[]{:S(2)}) collective-permute-start(f16[128,512]{1,0:T(8,128)(2,1)S(1)} %add_convert_fusion.8), channel_id=1, source_target_pairs={{0,2},{2,4},{4,6},{6,8},{8,10},{10,12},{12,14},{14,0},{1,3},{3,5},... | collective-permute-start | bytes 393224 | tf_op jit(solution)/shard_map/ppermute | solution.py:188
  85.6 6.0 %collective-permute-start.21 = (f16[128,512]{1,0:T(8,128)(2,1)S(1)}, f16[128,512]{1,0:T(8,128)(2,1)S(1)}, u32[]{:S(2)}, u32[]{:S(2)}) collective-permute-start(f16[128,512]{1,0:T(8,128)(2,1)S(1)} %add_convert_fusion.7), channel_id=1, source_target_pairs={{0,14},{2,0},{4,2},{6,4},{8,6},{10,8},{12,10},{14,12},{1,15},{3,1}... | collective-permute-start | bytes 393224 | tf_op jit(solution)/shard_map/ppermute | solution.py:188
  88.3 6.0 %collective-permute-start.26 = (f16[128,512]{1,0:T(8,128)(2,1)S(1)}, f16[128,512]{1,0:T(8,128)(2,1)S(1)}, u32[]{:S(2)}, u32[]{:S(2)}) collective-permute-start(f16[128,512]{1,0:T(8,128)(2,1)S(1)} %add_convert_fusion.2), channel_id=1, source_target_pairs={{0,2},{2,4},{4,6},{6,8},{8,10},{10,12},{12,14},{14,0},{1,3},{3,5},... | collective-permute-start | bytes 393224 | tf_op jit(solution)/shard_map/ppermute | solution.py:188
  88.7 5.7 %collective-permute-start.19 = (f16[128,512]{1,0:T(8,128)(2,1)S(1)}, f16[128,512]{1,0:T(8,128)(2,1)S(1)}, u32[]{:S(2)}, u32[]{:S(2)}) collective-permute-start(f16[128,512]{1,0:T(8,128)(2,1)S(1)} %add_convert_fusion.9), channel_id=1, source_target_pairs={{0,14},{2,0},{4,2},{6,4},{8,6},{10,8},{12,10},{14,12},{1,15},{3,1}... | collective-permute-start | bytes 393224 | tf_op jit(solution)/shard_map/ppermute | solution.py:188
  91.5 5.6 %collective-permute-start.23 = (f16[128,512]{1,0:T(8,128)(2,1)S(1)}, f16[128,512]{1,0:T(8,128)(2,1)S(1)}, u32[]{:S(2)}, u32[]{:S(2)}) collective-permute-start(f16[128,512]{1,0:T(8,128)(2,1)S(1)} %add_convert_fusion.5), channel_id=1, source_target_pairs={{0,2},{2,4},{4,6},{6,8},{8,10},{10,12},{12,14},{14,0},{1,3},{3,5},... | collective-permute-start | bytes 393224 | tf_op jit(solution)/shard_map/ppermute | solution.py:188
  91.6 5.6 %collective-permute-start.28 = (f16[128,512]{1,0:T(8,128)(2,1)S(1)}, f16[128,512]{1,0:T(8,128)(2,1)S(1)}, u32[]{:S(2)}, u32[]{:S(2)}) collective-permute-start(f16[128,512]{1,0:T(8,128)(2,1)S(1)} %add_convert_fusion.4), channel_id=1, source_target_pairs={{0,14},{2,0},{4,2},{6,4},{8,6},{10,8},{12,10},{14,12},{1,15},{3,1}... | collective-permute-start | bytes 393224 | tf_op jit(solution)/shard_map/ppermute | solution.py:188
  94.5 37.8 %copy-start.2 = (s32[8,64]{1,0:T(8,128)S(1)}, s32[8,64]{1,0:T(8,128)}, u32[]{:S(2)}) copy-start(s32[8,64]{1,0:T(8,128)} %get-tuple-element.60.places_ref) | copy-start | bytes 6148
  94.5 5.8 %collective-permute-start.22 = (f16[128,512]{1,0:T(8,128)(2,1)S(1)}, f16[128,512]{1,0:T(8,128)(2,1)S(1)}, u32[]{:S(2)}, u32[]{:S(2)}) collective-permute-start(f16[128,512]{1,0:T(8,128)(2,1)S(1)} %get-tuple-element.105), channel_id=1, source_target_pairs={{0,14},{2,0},{4,2},{6,4},{8,6},{10,8},{12,10},{14,12},{1,15},{3,1}... | collective-permute-start | bytes 393224 | tf_op jit(solution)/shard_map/ppermute | solution.py:188
  97.0 7.9 %collective-permute-start.27 = (f16[128,512]{1,0:T(8,128)(2,1)S(1)}, f16[128,512]{1,0:T(8,128)(2,1)S(1)}, u32[]{:S(2)}, u32[]{:S(2)}) collective-permute-start(f16[128,512]{1,0:T(8,128)(2,1)S(1)} %get-tuple-element.113), channel_id=1, source_target_pairs={{0,2},{2,4},{4,6},{6,8},{8,10},{10,12},{12,14},{14,0},{1,3},{3,5},... | collective-permute-start | bytes 393224 | tf_op jit(solution)/shard_map/ppermute | solution.py:188
  97.1 7.7 %collective-permute-start.24 = (f16[128,512]{1,0:T(8,128)(2,1)S(1)}, f16[128,512]{1,0:T(8,128)(2,1)S(1)}, u32[]{:S(2)}, u32[]{:S(2)}) collective-permute-start(f16[128,512]{1,0:T(8,128)(2,1)S(1)} %add_convert_fusion.3), channel_id=1, source_target_pairs={{0,2},{2,4},{4,6},{6,8},{8,10},{10,12},{12,14},{14,0},{1,3},{3,5},... | collective-permute-start | bytes 393224 | tf_op jit(solution)/shard_map/ppermute | solution.py:188
  97.3 7.6 %collective-permute-start.29 = (f16[128,512]{1,0:T(8,128)(2,1)S(1)}, f16[128,512]{1,0:T(8,128)(2,1)S(1)}, u32[]{:S(2)}, u32[]{:S(2)}) collective-permute-start(f16[128,512]{1,0:T(8,128)(2,1)S(1)} %add_convert_fusion), channel_id=1, source_target_pairs={{0,14},{2,0},{4,2},{6,4},{8,6},{10,8},{12,10},{14,12},{1,15},{3,1}... | collective-permute-start | bytes 393224 | tf_op jit(solution)/shard_map/ppermute | solution.py:188
  107.0 12.5 %all-to-all-start.2 = ((f16[16,32,512]{2,1,0:T(8,128)(2,1)}), f16[16,32,512]{2,1,0:T(8,128)(2,1)S(1)}, u32[]{:S(2)}, u32[]{:S(2)}) async-start(f16[16,32,512]{2,1,0:T(8,128)(2,1)} %bitcast.5), calls=%async_computation.2 | async-start | bytes 1048576 | tf_op jit(solution)/shard_map/all_to_all | solution.py:322
  119.6 12.7 %collective-permute-start.30 = (f32[32,256]{1,0:T(8,128)S(1)}, f32[32,256]{1,0:T(8,128)S(1)}, u32[]{:S(2)}, u32[]{:S(2)}) collective-permute-start(f32[32,256]{1,0:T(8,128)S(1)} %get-tuple-element.115), channel_id=1, source_target_pairs={{0,1},{1,0},{2,3},{3,2},{4,5},{5,4},{6,7},{7,6},{8,9},{9,8},{10,11... | collective-permute-start | bytes 98312 | tf_op jit(solution)/shard_map/ppermute | solution.py:184
where the time goes:
time: 134 us
  starting transfers between devices  59.1 us (44%)
  blocking collectives  38.4 us (29%)
  waiting for transfers between devices  18 us (13%)
  Pallas kernels  11.2 us (8%)
  other arithmetic  4.8 us (4%)
  between operations  1.62 us (1%)
    ppermute x28, starting transfers between devices, pass_on(): return lax.ppermute(x, 'z', [(i, (i + by) % DEEP) for i in range(DEEP)])  40.1 us
    all_to_all x1, blocking collectives, local(): stats = lax.all_to_all(stats, CHIPS, 0, 0, tiled=True)  21 us
    all_to_all x1, blocking collectives, local(): lax.all_to_all(jnp.broadcast_to(slots[None], (SEQS,) + slots.shape), PLAN...  17.4 us
    ppermute x3, starting transfers between devices, swap_cores(): return lax.ppermute(x, 'c', [(0, 1), (1, 0)])  15.4 us
    all_to_all x1, waiting for transfers between devices, local(): back = lax.all_to_all(back, PLANE, 0, 0, tiled=True)  8.95 us
    ppermute x28, waiting for transfers between devices, pass_on(): return lax.ppermute(x, 'z', [(i, (i + by) % DEEP) for i in range(DEEP)])  7.14 us
    all_to_all x1, starting transfers between devices, local(): back = lax.all_to_all(back, PLANE, 0, 0, tiled=True)  3.57 us
  transfers between devices with their start and end apart: 32, of which 9 were waited for; matrix products, arithmetic and copies ran while one was open for 2% of the time, Pallas kernels for 2%

commit v1 on v0

--- a/solution.py
+++ b/solution.py
@@ -251,7 +251,8 @@
     got = swap_cores(give)
 
     slots = jnp.concatenate([keep, got, aux], axis=1)
-    slots, own_weight = lax.optimization_barrier((slots, own_weight))
+    counts = jnp.maximum(lax.optimization_barrier((counts, give))[0], 0)
+    slots, own_weight, counts = lax.optimization_barrier((slots, own_weight, counts))
     near_t = swap_cores(own_weight).T
     slots = lax.all_to_all(jnp.broadcast_to(slots[None], (SEQS,) + slots.shape), PLANE, 0, 0, tiled=True)
     low, high, row_data = pl.pallas_call(

time: 134 us -> 134 us (level)
  transfers between devices with their start and end apart: 32 -> 32, of which waited for: 9 -> 9; matrix products, arithmetic and copies ran while one was open for 2% -> 3% of each run, Pallas kernels for 2% -> 2%
where the time goes in v1:
time: 134 us; the launch traced here: 133 us
  starting transfers between devices  59.7 us (45%)
  blocking collectives  38.4 us (29%)
  waiting for transfers between devices  17.3 us (13%)
  Pallas kernels  11.3 us (8%)
  other arithmetic  5.38 us (4%)
    ppermute x28, starting transfers between devices, pass_on(): return lax.ppermute(x, 'z', [(i, (i + by) % DEEP) for i in range(DEEP)])  40.7 us
    all_to_all x1, blocking collectives, local(): stats = lax.all_to_all(stats, CHIPS, 0, 0, tiled=True)  21 us
    all_to_all x1, blocking collectives, local(): lax.all_to_all(jnp.broadcast_to(slots[None], (SEQS,) + slots.shape), PLAN...  17.4 us
    ppermute x3, starting transfers between devices, swap_cores(): return lax.ppermute(x, 'c', [(0, 1), (1, 0)])  15.4 us
    all_to_all x1, waiting for transfers between devices, local(): back = lax.all_to_all(back, PLANE, 0, 0, tiled=True)  8.95 us
    ppermute x28, waiting for transfers between devices, pass_on(): return lax.ppermute(x, 'z', [(i, (i + by) % DEEP) for i in range(DEEP)])  7.13 us
    all_to_all x1, starting transfers between devices, local(): back = lax.all_to_all(back, PLANE, 0, 0, tiled=True)  3.57 us
  transfers between devices with their start and end apart: 32, of which 9 were waited for; matrix products, arithmetic and copies ran while one was open for 3% of the time, Pallas kernels for 2%

profile of v1, /device:TPU:1, one launch (start us, length us, event | category | flops | bytes accessed | tf_op | source)
XLA Modules:
  0.0 133.2 jit_solution(16594225638904516244)
XLA Ops:
  0.7 2.0 %shard_map.64 = (bf16[32,256]{1,0:T(8,128)(2,1)}, bf16[32,128]{1,0:T(8,128)(2,1)}, bf16[32,256]{1,0:T(8,128)(2,1)}, s32[8,64]{1,0:T(8,128)}) custom-call(s32[16]{0:T(128)} %counts_ref.1, s32[1]{0:T(128)S(6)} %copy.7.ratio_ref, s32[1,1024]{1,0:T(1,128)} %positions_ref.1, s32[1,1024]{1,0:T(1,128)} %targets_ref.1, bf16[1024,256]{1,0:T(8,128)(2,1)} %bitcast.15), custom_call_target="tpu_custom_call" | custom-call | tf_op jit(solution)/shard_map/pallas_call | solution.py:239
  2.6 3.2 %collective-permute-start = (bf16[32,256]{1,0:T(8,128)(2,1)}, bf16[32,256]{1,0:T(8,128)(2,1)S(1)}, u32[]{:S(2)}, u32[]{:S(2)}) collective-permute-start(bf16[32,256]{1,0:T(8,128)(2,1)} %get-tuple-element.64), channel_id=1, source_target_pairs={{0,1},{1,0},{2,3},{3,2},{4,5},{5,4},{6,7},{7,6},{8,9},{9,8},{10,11... | collective-permute-start | bytes 49160 | tf_op jit(solution)/shard_map/ppermute | solution.py:184
  5.9 0.7 broadcast_maximum_fusion.counts_ref
  6.5 0.4 collective-permute-done
  6.9 0.7 pad_maximum_fusion
  7.7 0.3 collective-permute-start.7
  8.0 0.1 broadcast_in_dim.13
  8.1 17.4 %all_to_all.15 = bf16[16,32,640]{2,1,0:T(8,128)(2,1)S(1)} all-to-all(bf16[16,32,640]{2,1,0:T(8,128)(2,1)S(1)} %broadcast_in_dim.13), channel_id=1, replica_groups=mesh['y'=4,'x'=4,'z'=8,'c'=2] {'y','x'}, dimensions={0} | all-to-all | bytes 1310720 | tf_op jit(solution)/shard_map/all_to_all | solution.py:257
  25.5 1.0 shard_map.65
  26.5 1.7 %collective-permute-start.1 = (bf16[128,512]{1,0:T(8,128)(2,1)S(1)}, bf16[128,512]{1,0:T(8,128)(2,1)S(1)}, u32[]{:S(2)}, u32[]{:S(2)}) collective-permute-start(bf16[128,512]{1,0:T(8,128)(2,1)S(1)} %get-tuple-element.70.refs_0_), channel_id=1, source_target_pairs={{0,2},{2,4},{4,6},{6,8},{8,10},{10,12},{12,14},{14,0},{1,3},{3,5},... | collective-permute-start | bytes 393224 | tf_op jit(solution)/shard_map/ppermute | solution.py:188
  28.2 4.0 %collective-permute-start.4 = (bf16[128,512]{1,0:T(8,128)(2,1)S(1)}, bf16[128,512]{1,0:T(8,128)(2,1)S(1)}, u32[]{:S(2)}, u32[]{:S(2)}) collective-permute-start(bf16[128,512]{1,0:T(8,128)(2,1)S(1)} %get-tuple-element.71.refs_1_), channel_id=1, source_target_pairs={{0,14},{2,0},{4,2},{6,4},{8,6},{10,8},{12,10},{14,12},{1,15},{3,1}... | collective-permute-start | bytes 393224 | tf_op jit(solution)/shard_map/ppermute | solution.py:188
  32.2 1.4 %collective-permute-start.8 = (bf16[128,512]{1,0:T(8,128)(2,1)S(1)}, bf16[128,512]{1,0:T(8,128)(2,1)S(1)}, u32[]{:S(2)}, u32[]{:S(2)}) collective-permute-start(bf16[128,512]{1,0:T(8,128)(2,1)S(1)} %get-tuple-element.70.refs_0_), channel_id=1, source_target_pairs={{0,14},{2,0},{4,2},{6,4},{8,6},{10,8},{12,10},{14,12},{1,15},{3,1}... | collective-permute-start | bytes 393224 | tf_op jit(solution)/shard_map/ppermute | solution.py:188
  33.6 0.1 collective-permute-start.9
  33.7 0.8 collective-permute-done.1.refs_4_
  34.5 2.8 %collective-permute-start.5 = (bf16[128,512]{1,0:T(8,128)(2,1)S(1)}, bf16[128,512]{1,0:T(8,128)(2,1)S(1)}, u32[]{:S(2)}, u32[]{:S(2)}) collective-permute-start(bf16[128,512]{1,0:T(8,128)(2,1)S(1)} %collective-permute-done.4.refs_3_), channel_id=1, source_target_pairs={{0,14},{2,0},{4,2},{6,4},{8,6},{10,8},{12,10},{14,12},{1,15},{3,1}... | collective-permute-start | bytes 393224 | tf_op jit(solution)/shard_map/ppermute | solution.py:188
  37.2 2.7 %collective-permute-start.10 = (bf16[128,512]{1,0:T(8,128)(2,1)S(1)}, bf16[128,512]{1,0:T(8,128)(2,1)S(1)}, u32[]{:S(2)}, u32[]{:S(2)}) collective-permute-start(bf16[128,512]{1,0:T(8,128)(2,1)S(1)} %collective-permute-done.8.refs_2_), channel_id=1, source_target_pairs={{0,14},{2,0},{4,2},{6,4},{8,6},{10,8},{12,10},{14,12},{1,15},{3,1}... | collective-permute-start | bytes 393224 | tf_op jit(solution)/shard_map/ppermute | solution.py:188
  39.9 0.0 collective-permute-done.9.refs_5_
  39.9 0.5 collective-permute-done.2.refs_8_
  40.5 0.0 collective-permute-start.3
  40.5 0.0 collective-permute-done.5.refs_7_
  40.5 2.7 %collective-permute-start.6 = (bf16[128,512]{1,0:T(8,128)(2,1)S(1)}, bf16[128,512]{1,0:T(8,128)(2,1)S(1)}, u32[]{:S(2)}, u32[]{:S(2)}) collective-permute-start(bf16[128,512]{1,0:T(8,128)(2,1)S(1)} %collective-permute-done.5.refs_7_), channel_id=1, source_target_pairs={{0,14},{2,0},{4,2},{6,4},{8,6},{10,8},{12,10},{14,12},{1,15},{3,1}... | collective-permute-start | bytes 393224 | tf_op jit(solution)/shard_map/ppermute | solution.py:188
  43.2 0.0 collective-permute-done.10.refs_6_
  43.2 2.2 %collective-permute-start.12 = (bf16[128,512]{1,0:T(8,128)(2,1)S(1)}, bf16[128,512]{1,0:T(8,128)(2,1)S(1)}, u32[]{:S(2)}, u32[]{:S(2)}) collective-permute-start(bf16[128,512]{1,0:T(8,128)(2,1)S(1)} %collective-permute-done.10.refs_6_), channel_id=1, source_target_pairs={{0,14},{2,0},{4,2},{6,4},{8,6},{10,8},{12,10},{14,12},{1,15},{3,1}... | collective-permute-start | bytes 393224 | tf_op jit(solution)/shard_map/ppermute | solution.py:188
  45.4 0.0 collective-permute-done.11.refs_9_
  45.4 0.0 collective-permute-start.13
  45.4 1.0 collective-permute-done.3.refs_2_
  46.4 0.1 collective-permute-done.6.refs_1_
  46.5 0.6 collective-permute-start.14
  47.1 2.7 %collective-permute-start.15 = (bf16[128,512]{1,0:T(8,128)(2,1)S(1)}, bf16[128,512]{1,0:T(8,128)(2,1)S(1)}, u32[]{:S(2)}, u32[]{:S(2)}) collective-permute-start(bf16[128,512]{1,0:T(8,128)(2,1)S(1)} %collective-permute-done.6.refs_1_), channel_id=1, source_target_pairs={{0,14},{2,0},{4,2},{6,4},{8,6},{10,8},{12,10},{14,12},{1,15},{3,1}... | collective-permute-start | bytes 393224 | tf_op jit(solution)/shard_map/ppermute | solution.py:188
  49.8 2.4 %select_bitcast_fusion.own_ref = bf16[494,4096]{1,0:T(8,128)(2,1)S(1)} fusion(bf16[4096,494]{0,1:T(8,128)(2,1)} %param.11, pred[]{:T(512)} %bitcast.1), kind=kLoop, calls=%fused_computation | loop fusion | flops 2023424 | bytes 8093697 | tf_op jit(solution)/shard_map/transpose | solution.py:273
  52.2 0.0 collective-permute-done.7
  52.3 1.5 %shard_map.66 = (f32[512,256]{1,0:T(8,128)S(1)}, f32[512,256]{1,0:T(8,128)S(1)}) custom-call(bf16[494,4096]{1,0:T(8,128)(2,1)S(1)} %select_bitcast_fusion.own_ref, bf16[494,4096]{1,0:T(8,128)(2,1)S(1)} %bitcast.9, bf16[128,512]{1,0:T(8,128)(2,1)S(1)} %get-tuple-element.70.refs_0_, bf16[128,512]{1,0:T(8,128)(2,1)S(1)} %get-tuple-element.71.refs_1_, ...), custom_call_target="tpu_custom_call" | custom-call | tf_op jit(solution)/shard_map/pallas_call | solution.py:276
  53.8 0.0 collective-permute-done.12.refs_0_
  53.8 0.0 collective-permute-done.14.refs_4_
  53.8 0.0 collective-permute-done.15.refs_5_
  53.8 1.2 shard_map.67
  55.1 21.0 %all_to_all.16.stats_ref = f32[128,2,256]{2,1,0:T(2,128)S(1)} all-to-all(f32[128,2,256]{2,1,0:T(2,128)S(1)} %get-tuple-element.75), channel_id=1, replica_groups=mesh['y'=4,'x'=4,'z'=8,'c'=2] {'y','x','z'}, dimensions={0} | all-to-all | bytes 524288 | tf_op jit(solution)/shard_map/all_to_all | solution.py:291
  76.1 1.4 %shard_map.68 = (bf16[256,512]{1,0:T(8,128)(2,1)S(1)}, bf16[256,512]{1,0:T(8,128)(2,1)S(1)}, f32[128,512]{1,0:T(8,128)S(1)}, f32[128,512]{1,0:T(8,128)S(1)}, f32...) custom-call(f32[128,2,256]{2,1,0:T(2,128)S(1)} %all_to_all.16.stats_ref, ...), custom_call_target="tpu_custom_call" | custom-call | tf_op jit(solution)/shard_map/pallas_call | solution.py:295
  77.5 1.6 %shard_map.69 = (f32[128,512]{1,0:T(8,128)S(1)}, f32[128,512]{1,0:T(8,128)S(1)}, f32[128,512]{1,0:T(8,128)S(1)}, f32[128,512]{1,0:T(8,128)S(1)}, f32[128,512]{1,...) custom-call(bf16[256,512]{1,0:T(8,128)(2,1)S(1)} %get-tuple-element., ...), custom_call_target="tpu_custom_call" | custom-call | tf_op jit(solution)/shard_map/pallas_call | solution.py:302
  79.1 0.4 collective-permute-start.17
  79.5 2.5 %collective-permute-start.18 = (f16[128,512]{1,0:T(8,128)(2,1)S(1)}, f16[128,512]{1,0:T(8,128)(2,1)S(1)}, u32[]{:S(2)}, u32[]{:S(2)}) collective-permute-start(f16[128,512]{1,0:T(8,128)(2,1)S(1)} %convert_element_type.94), channel_id=1, source_target_pairs={{0,14},{2,0},{4,2},{6,4},{8,6},{10,8},{12,10},{14,12},{1,15},{3,1}... | collective-permute-start | bytes 393224 | tf_op jit(solution)/shard_map/ppermute | solution.py:188
  82.0 2.7 %collective-permute-start.16 = (f16[128,512]{1,0:T(8,128)(2,1)S(1)}, f16[128,512]{1,0:T(8,128)(2,1)S(1)}, u32[]{:S(2)}, u32[]{:S(2)}) collective-permute-start(f16[128,512]{1,0:T(8,128)(2,1)S(1)} %convert_element_type.92), channel_id=1, source_target_pairs={{0,14},{2,0},{4,2},{6,4},{8,6},{10,8},{12,10},{14,12},{1,15},{3,1}... | collective-permute-start | bytes 393224 | tf_op jit(solution)/shard_map/ppermute | solution.py:188
  84.8 0.1 collective-permute-start.20
  85.0 2.7 %collective-permute-start.21 = (f16[128,512]{1,0:T(8,128)(2,1)S(1)}, f16[128,512]{1,0:T(8,128)(2,1)S(1)}, u32[]{:S(2)}, u32[]{:S(2)}) collective-permute-start(f16[128,512]{1,0:T(8,128)(2,1)S(1)} %add_convert_fusion.7), channel_id=1, source_target_pairs={{0,14},{2,0},{4,2},{6,4},{8,6},{10,8},{12,10},{14,12},{1,15},{3,1}... | collective-permute-start | bytes 393224 | tf_op jit(solution)/shard_map/ppermute | solution.py:188
  87.7 0.3 collective-permute-start.26
  88.1 2.7 %collective-permute-start.19 = (f16[128,512]{1,0:T(8,128)(2,1)S(1)}, f16[128,512]{1,0:T(8,128)(2,1)S(1)}, u32[]{:S(2)}, u32[]{:S(2)}) collective-permute-start(f16[128,512]{1,0:T(8,128)(2,1)S(1)} %add_convert_fusion.9), channel_id=1, source_target_pairs={{0,14},{2,0},{4,2},{6,4},{8,6},{10,8},{12,10},{14,12},{1,15},{3,1}... | collective-permute-start | bytes 393224 | tf_op jit(solution)/shard_map/ppermute | solution.py:188
  90.9 0.1 collective-permute-start.23
  91.0 2.7 %collective-permute-start.28 = (f16[128,512]{1,0:T(8,128)(2,1)S(1)}, f16[128,512]{1,0:T(8,128)(2,1)S(1)}, u32[]{:S(2)}, u32[]{:S(2)}) collective-permute-start(f16[128,512]{1,0:T(8,128)(2,1)S(1)} %add_convert_fusion.4), channel_id=1, source_target_pairs={{0,14},{2,0},{4,2},{6,4},{8,6},{10,8},{12,10},{14,12},{1,15},{3,1}... | collective-permute-start | bytes 393224 | tf_op jit(solution)/shard_map/ppermute | solution.py:188
  93.8 0.1 add_convert_fusion.1
  93.9 2.6 %collective-permute-start.22 = (f16[128,512]{1,0:T(8,128)(2,1)S(1)}, f16[128,512]{1,0:T(8,128)(2,1)S(1)}, u32[]{:S(2)}, u32[]{:S(2)}) collective-permute-start(f16[128,512]{1,0:T(8,128)(2,1)S(1)} %get-tuple-element.109), channel_id=1, source_target_pairs={{0,14},{2,0},{4,2},{6,4},{8,6},{10,8},{12,10},{14,12},{1,15},{3,1}... | collective-permute-start | bytes 393224 | tf_op jit(solution)/shard_map/ppermute | solution.py:188
  96.4 0.1 collective-permute-done.23
  96.6 0.1 collective-permute-start.24
  96.7 3.0 %collective-permute-start.29 = (f16[128,512]{1,0:T(8,128)(2,1)S(1)}, f16[128,512]{1,0:T(8,128)(2,1)S(1)}, u32[]{:S(2)}, u32[]{:S(2)}) collective-permute-start(f16[128,512]{1,0:T(8,128)(2,1)S(1)} %add_convert_fusion), channel_id=1, source_target_pairs={{0,14},{2,0},{4,2},{6,4},{8,6},{10,8},{12,10},{14,12},{1,15},{3,1}... | collective-permute-start | bytes 393224 | tf_op jit(solution)/shard_map/ppermute | solution.py:188
  99.7 4.6 %collective-permute-done.24 = f16[128,512]{1,0:T(8,128)(2,1)S(1)} collective-permute-done((f16[128,512]{1,0:T(8,128)(2,1)S(1)}, f16[128,512]{1,0:T(8,128)(2,1)S(1)}, u32[]{:S(2)}, u32[]{:S(2)}) %collective-permute-start.24) | collective-permute-done | bytes 131104 | tf_op jit(solution)/shard_map/ppermute | solution.py:188
  104.2 0.1 convert_add_fusion.1.low_ref
  104.3 0.1 convert_add_fusion.high_ref
  104.4 1.1 shard_map.70
  105.5 0.9 convert_element_type.120
  106.4 3.6 %all-to-all-start.2 = ((f16[16,32,512]{2,1,0:T(8,128)(2,1)}), f16[16,32,512]{2,1,0:T(8,128)(2,1)S(1)}, u32[]{:S(2)}, u32[]{:S(2)}) async-start(f16[16,32,512]{2,1,0:T(8,128)(2,1)} %bitcast.5), calls=%async_computation.2 | async-start | bytes 1048576 | tf_op jit(solution)/shard_map/all_to_all | solution.py:323
  109.9 8.9 %all-to-all-done.2 = f16[16,32,512]{2,1,0:T(8,128)(2,1)S(1)} async-done(((f16[16,32,512]{2,1,0:T(8,128)(2,1)}), f16[16,32,512]{2,1,0:T(8,128)(2,1)S(1)}, u32[]{:S(2)}, u32[]{:S(2)}) %all-to-all-start.2) | async-done | bytes 524320 | tf_op jit(solution)/shard_map/all_to_all | solution.py:323
  118.9 0.1 convert_reduce_fusion
  119.0 11.8 %collective-permute-start.30 = (f32[32,256]{1,0:T(8,128)S(1)}, f32[32,256]{1,0:T(8,128)S(1)}, u32[]{:S(2)}, u32[]{:S(2)}) collective-permute-start(f32[32,256]{1,0:T(8,128)S(1)} %get-tuple-element.119), channel_id=1, source_target_pairs={{0,1},{1,0},{2,3},{3,2},{4,5},{5,4},{6,7},{7,6},{8,9},{9,8},{10,11... | collective-permute-start | bytes 98312 | tf_op jit(solution)/shard_map/ppermute | solution.py:184
  130.8 0.9 collective-permute-done.30.got_ref
  131.7 1.5 %shard_map.71 = f32[1024,256]{1,0:T(8,128)} custom-call(s32[8,64]{1,0:T(8,128)S(1)} %copy-done, f32[32,256]{1,0:T(8,128)S(1)} %get-tuple-element.120.kept_ref, f32[32,256]{1,0:T(8,128)S(1)} %collective-permute-done.30.got_ref), custom_call_target="tpu_custom_call" | custom-call | tf_op jit(solution)/shard_map/pallas_call | solution.py:327
  (35 shorter events, 0.5 us)
Async XLA Ops:
  2.6 4.3 %collective-permute-start = (bf16[32,256]{1,0:T(8,128)(2,1)}, bf16[32,256]{1,0:T(8,128)(2,1)S(1)}, u32[]{:S(2)}, u32[]{:S(2)}) collective-permute-start(bf16[32,256]{1,0:T(8,128)(2,1)} %get-tuple-element.64), channel_id=1, source_target_pairs={{0,1},{1,0},{2,3},{3,2},{4,5},{5,4},{6,7},{7,6},{8,9},{9,8},{10,11... | collective-permute-start | bytes 49160 | tf_op jit(solution)/shard_map/ppermute | solution.py:184
  7.7 44.6 %collective-permute-start.7 = (bf16[4096,494]{0,1:T(8,128)(2,1)}, bf16[4096,494]{0,1:T(8,128)(2,1)S(1)}, u32[]{:S(2)}, u32[]{:S(2)}) collective-permute-start(bf16[4096,494]{0,1:T(8,128)(2,1)} %param.11), channel_id=1, source_target_pairs={{0,1},{1,0},{2,3},{3,2},{4,5},{5,4},{6,7},{7,6},{8,9},{9,8},{10,11... | collective-permute-start | bytes 12140552 | tf_op jit(solution)/shard_map/ppermute | solution.py:184
  26.5 8.0 %collective-permute-start.1 = (bf16[128,512]{1,0:T(8,128)(2,1)S(1)}, bf16[128,512]{1,0:T(8,128)(2,1)S(1)}, u32[]{:S(2)}, u32[]{:S(2)}) collective-permute-start(bf16[128,512]{1,0:T(8,128)(2,1)S(1)} %get-tuple-element.70.refs_0_), channel_id=1, source_target_pairs={{0,2},{2,4},{4,6},{6,8},{8,10},{10,12},{12,14},{14,0},{1,3},{3,5},... | collective-permute-start | bytes 393224 | tf_op jit(solution)/shard_map/ppermute | solution.py:188
  28.2 6.3 %collective-permute-start.4 = (bf16[128,512]{1,0:T(8,128)(2,1)S(1)}, bf16[128,512]{1,0:T(8,128)(2,1)S(1)}, u32[]{:S(2)}, u32[]{:S(2)}) collective-permute-start(bf16[128,512]{1,0:T(8,128)(2,1)S(1)} %get-tuple-element.71.refs_1_), channel_id=1, source_target_pairs={{0,14},{2,0},{4,2},{6,4},{8,6},{10,8},{12,10},{14,12},{1,15},{3,1}... | collective-permute-start | bytes 393224 | tf_op jit(solution)/shard_map/ppermute | solution.py:188
  32.2 5.0 %collective-permute-start.8 = (bf16[128,512]{1,0:T(8,128)(2,1)S(1)}, bf16[128,512]{1,0:T(8,128)(2,1)S(1)}, u32[]{:S(2)}, u32[]{:S(2)}) collective-permute-start(bf16[128,512]{1,0:T(8,128)(2,1)S(1)} %get-tuple-element.70.refs_0_), channel_id=1, source_target_pairs={{0,14},{2,0},{4,2},{6,4},{8,6},{10,8},{12,10},{14,12},{1,15},{3,1}... | collective-permute-start | bytes 393224 | tf_op jit(solution)/shard_map/ppermute | solution.py:188
  33.6 6.4 %collective-permute-start.9 = (bf16[128,512]{1,0:T(8,128)(2,1)S(1)}, bf16[128,512]{1,0:T(8,128)(2,1)S(1)}, u32[]{:S(2)}, u32[]{:S(2)}) collective-permute-start(bf16[128,512]{1,0:T(8,128)(2,1)S(1)} %get-tuple-element.71.refs_1_), channel_id=1, source_target_pairs={{0,2},{2,4},{4,6},{6,8},{8,10},{10,12},{12,14},{14,0},{1,3},{3,5},... | collective-permute-start | bytes 393224 | tf_op jit(solution)/shard_map/ppermute | solution.py:188
  34.5 6.0 %collective-permute-start.2 = (bf16[128,512]{1,0:T(8,128)(2,1)S(1)}, bf16[128,512]{1,0:T(8,128)(2,1)S(1)}, u32[]{:S(2)}, u32[]{:S(2)}) collective-permute-start(bf16[128,512]{1,0:T(8,128)(2,1)S(1)} %collective-permute-done.1.refs_4_), channel_id=1, source_target_pairs={{0,2},{2,4},{4,6},{6,8},{8,10},{10,12},{12,14},{14,0},{1,3},{3,5},... | collective-permute-start | bytes 393224 | tf_op jit(solution)/shard_map/ppermute | solution.py:188
  34.5 6.0 %collective-permute-start.5 = (bf16[128,512]{1,0:T(8,128)(2,1)S(1)}, bf16[128,512]{1,0:T(8,128)(2,1)S(1)}, u32[]{:S(2)}, u32[]{:S(2)}) collective-permute-start(bf16[128,512]{1,0:T(8,128)(2,1)S(1)} %collective-permute-done.4.refs_3_), channel_id=1, source_target_pairs={{0,14},{2,0},{4,2},{6,4},{8,6},{10,8},{12,10},{14,12},{1,15},{3,1}... | collective-permute-start | bytes 393224 | tf_op jit(solution)/shard_map/ppermute | solution.py:188
  37.2 6.0 %collective-permute-start.10 = (bf16[128,512]{1,0:T(8,128)(2,1)S(1)}, bf16[128,512]{1,0:T(8,128)(2,1)S(1)}, u32[]{:S(2)}, u32[]{:S(2)}) collective-permute-start(bf16[128,512]{1,0:T(8,128)(2,1)S(1)} %collective-permute-done.8.refs_2_), channel_id=1, source_target_pairs={{0,14},{2,0},{4,2},{6,4},{8,6},{10,8},{12,10},{14,12},{1,15},{3,1}... | collective-permute-start | bytes 393224 | tf_op jit(solution)/shard_map/ppermute | solution.py:188
  39.9 5.4 %collective-permute-start.11 = (bf16[128,512]{1,0:T(8,128)(2,1)S(1)}, bf16[128,512]{1,0:T(8,128)(2,1)S(1)}, u32[]{:S(2)}, u32[]{:S(2)}) collective-permute-start(bf16[128,512]{1,0:T(8,128)(2,1)S(1)} %collective-permute-done.9.refs_5_), channel_id=1, source_target_pairs={{0,2},{2,4},{4,6},{6,8},{8,10},{10,12},{12,14},{14,0},{1,3},{3,5},... | collective-permute-start | bytes 393224 | tf_op jit(solution)/shard_map/ppermute | solution.py:188
  40.5 5.9 %collective-permute-start.3 = (bf16[128,512]{1,0:T(8,128)(2,1)S(1)}, bf16[128,512]{1,0:T(8,128)(2,1)S(1)}, u32[]{:S(2)}, u32[]{:S(2)}) collective-permute-start(bf16[128,512]{1,0:T(8,128)(2,1)S(1)} %collective-permute-done.2.refs_8_), channel_id=1, source_target_pairs={{0,2},{2,4},{4,6},{6,8},{8,10},{10,12},{12,14},{14,0},{1,3},{3,5},... | collective-permute-start | bytes 393224 | tf_op jit(solution)/shard_map/ppermute | solution.py:188
  40.5 6.0 %collective-permute-start.6 = (bf16[128,512]{1,0:T(8,128)(2,1)S(1)}, bf16[128,512]{1,0:T(8,128)(2,1)S(1)}, u32[]{:S(2)}, u32[]{:S(2)}) collective-permute-start(bf16[128,512]{1,0:T(8,128)(2,1)S(1)} %collective-permute-done.5.refs_7_), channel_id=1, source_target_pairs={{0,14},{2,0},{4,2},{6,4},{8,6},{10,8},{12,10},{14,12},{1,15},{3,1}... | collective-permute-start | bytes 393224 | tf_op jit(solution)/shard_map/ppermute | solution.py:188
  43.2 10.6 %collective-permute-start.12 = (bf16[128,512]{1,0:T(8,128)(2,1)S(1)}, bf16[128,512]{1,0:T(8,128)(2,1)S(1)}, u32[]{:S(2)}, u32[]{:S(2)}) collective-permute-start(bf16[128,512]{1,0:T(8,128)(2,1)S(1)} %collective-permute-done.10.refs_6_), channel_id=1, source_target_pairs={{0,14},{2,0},{4,2},{6,4},{8,6},{10,8},{12,10},{14,12},{1,15},{3,1}... | collective-permute-start | bytes 393224 | tf_op jit(solution)/shard_map/ppermute | solution.py:188
  45.4 8.4 %collective-permute-start.13 = (bf16[128,512]{1,0:T(8,128)(2,1)S(1)}, bf16[128,512]{1,0:T(8,128)(2,1)S(1)}, u32[]{:S(2)}, u32[]{:S(2)}) collective-permute-start(bf16[128,512]{1,0:T(8,128)(2,1)S(1)} %collective-permute-done.11.refs_9_), channel_id=1, source_target_pairs={{0,2},{2,4},{4,6},{6,8},{8,10},{10,12},{12,14},{14,0},{1,3},{3,5},... | collective-permute-start | bytes 393224 | tf_op jit(solution)/shard_map/ppermute | solution.py:188
  46.5 7.3 %collective-permute-start.14 = (bf16[128,512]{1,0:T(8,128)(2,1)S(1)}, bf16[128,512]{1,0:T(8,128)(2,1)S(1)}, u32[]{:S(2)}, u32[]{:S(2)}) collective-permute-start(bf16[128,512]{1,0:T(8,128)(2,1)S(1)} %collective-permute-done.3.refs_2_), channel_id=1, source_target_pairs={{0,2},{2,4},{4,6},{6,8},{8,10},{10,12},{12,14},{14,0},{1,3},{3,5},... | collective-permute-start | bytes 393224 | tf_op jit(solution)/shard_map/ppermute | solution.py:188
  47.1 6.7 %collective-permute-start.15 = (bf16[128,512]{1,0:T(8,128)(2,1)S(1)}, bf16[128,512]{1,0:T(8,128)(2,1)S(1)}, u32[]{:S(2)}, u32[]{:S(2)}) collective-permute-start(bf16[128,512]{1,0:T(8,128)(2,1)S(1)} %collective-permute-done.6.refs_1_), channel_id=1, source_target_pairs={{0,14},{2,0},{4,2},{6,4},{8,6},{10,8},{12,10},{14,12},{1,15},{3,1}... | collective-permute-start | bytes 393224 | tf_op jit(solution)/shard_map/ppermute | solution.py:188
  79.1 5.7 %collective-permute-start.17 = (f16[128,512]{1,0:T(8,128)(2,1)S(1)}, f16[128,512]{1,0:T(8,128)(2,1)S(1)}, u32[]{:S(2)}, u32[]{:S(2)}) collective-permute-start(f16[128,512]{1,0:T(8,128)(2,1)S(1)} %convert_element_type.93), channel_id=1, source_target_pairs={{0,2},{2,4},{4,6},{6,8},{8,10},{10,12},{12,14},{14,0},{1,3},{3,5},... | collective-permute-start | bytes 393224 | tf_op jit(solution)/shard_map/ppermute | solution.py:188
  79.5 5.4 %collective-permute-start.18 = (f16[128,512]{1,0:T(8,128)(2,1)S(1)}, f16[128,512]{1,0:T(8,128)(2,1)S(1)}, u32[]{:S(2)}, u32[]{:S(2)}) collective-permute-start(f16[128,512]{1,0:T(8,128)(2,1)S(1)} %convert_element_type.94), channel_id=1, source_target_pairs={{0,14},{2,0},{4,2},{6,4},{8,6},{10,8},{12,10},{14,12},{1,15},{3,1}... | collective-permute-start | bytes 393224 | tf_op jit(solution)/shard_map/ppermute | solution.py:188
  82.0 5.7 %collective-permute-start.25 = (f16[128,512]{1,0:T(8,128)(2,1)S(1)}, f16[128,512]{1,0:T(8,128)(2,1)S(1)}, u32[]{:S(2)}, u32[]{:S(2)}) collective-permute-start(f16[128,512]{1,0:T(8,128)(2,1)S(1)} %convert_element_type.111), channel_id=1, source_target_pairs={{0,2},{2,4},{4,6},{6,8},{8,10},{10,12},{12,14},{14,0},{1,3},{3,5},... | collective-permute-start | bytes 393224 | tf_op jit(solution)/shard_map/ppermute | solution.py:188
  82.0 6.0 %collective-permute-start.16 = (f16[128,512]{1,0:T(8,128)(2,1)S(1)}, f16[128,512]{1,0:T(8,128)(2,1)S(1)}, u32[]{:S(2)}, u32[]{:S(2)}) collective-permute-start(f16[128,512]{1,0:T(8,128)(2,1)S(1)} %convert_element_type.92), channel_id=1, source_target_pairs={{0,14},{2,0},{4,2},{6,4},{8,6},{10,8},{12,10},{14,12},{1,15},{3,1}... | collective-permute-start | bytes 393224 | tf_op jit(solution)/shard_map/ppermute | solution.py:188
  84.8 6.0 %collective-permute-start.20 = (f16[128,512]{1,0:T(8,128)(2,1)S(1)}, f16[128,512]{1,0:T(8,128)(2,1)S(1)}, u32[]{:S(2)}, u32[]{:S(2)}) collective-permute-start(f16[128,512]{1,0:T(8,128)(2,1)S(1)} %add_convert_fusion.8), channel_id=1, source_target_pairs={{0,2},{2,4},{4,6},{6,8},{8,10},{10,12},{12,14},{14,0},{1,3},{3,5},... | collective-permute-start | bytes 393224 | tf_op jit(solution)/shard_map/ppermute | solution.py:188
  85.0 6.0 %collective-permute-start.21 = (f16[128,512]{1,0:T(8,128)(2,1)S(1)}, f16[128,512]{1,0:T(8,128)(2,1)S(1)}, u32[]{:S(2)}, u32[]{:S(2)}) collective-permute-start(f16[128,512]{1,0:T(8,128)(2,1)S(1)} %add_convert_fusion.7), channel_id=1, source_target_pairs={{0,14},{2,0},{4,2},{6,4},{8,6},{10,8},{12,10},{14,12},{1,15},{3,1}... | collective-permute-start | bytes 393224 | tf_op jit(solution)/shard_map/ppermute | solution.py:188
  87.7 6.0 %collective-permute-start.26 = (f16[128,512]{1,0:T(8,128)(2,1)S(1)}, f16[128,512]{1,0:T(8,128)(2,1)S(1)}, u32[]{:S(2)}, u32[]{:S(2)}) collective-permute-start(f16[128,512]{1,0:T(8,128)(2,1)S(1)} %add_convert_fusion.2), channel_id=1, source_target_pairs={{0,2},{2,4},{4,6},{6,8},{8,10},{10,12},{12,14},{14,0},{1,3},{3,5},... | collective-permute-start | bytes 393224 | tf_op jit(solution)/shard_map/ppermute | solution.py:188
  88.1 5.7 %collective-permute-start.19 = (f16[128,512]{1,0:T(8,128)(2,1)S(1)}, f16[128,512]{1,0:T(8,128)(2,1)S(1)}, u32[]{:S(2)}, u32[]{:S(2)}) collective-permute-start(f16[128,512]{1,0:T(8,128)(2,1)S(1)} %add_convert_fusion.9), channel_id=1, source_target_pairs={{0,14},{2,0},{4,2},{6,4},{8,6},{10,8},{12,10},{14,12},{1,15},{3,1}... | collective-permute-start | bytes 393224 | tf_op jit(solution)/shard_map/ppermute | solution.py:188
  90.9 5.6 %collective-permute-start.23 = (f16[128,512]{1,0:T(8,128)(2,1)S(1)}, f16[128,512]{1,0:T(8,128)(2,1)S(1)}, u32[]{:S(2)}, u32[]{:S(2)}) collective-permute-start(f16[128,512]{1,0:T(8,128)(2,1)S(1)} %add_convert_fusion.5), channel_id=1, source_target_pairs={{0,2},{2,4},{4,6},{6,8},{8,10},{10,12},{12,14},{14,0},{1,3},{3,5},... | collective-permute-start | bytes 393224 | tf_op jit(solution)/shard_map/ppermute | solution.py:188
  91.0 5.6 %collective-permute-start.28 = (f16[128,512]{1,0:T(8,128)(2,1)S(1)}, f16[128,512]{1,0:T(8,128)(2,1)S(1)}, u32[]{:S(2)}, u32[]{:S(2)}) collective-permute-start(f16[128,512]{1,0:T(8,128)(2,1)S(1)} %add_convert_fusion.4), channel_id=1, source_target_pairs={{0,14},{2,0},{4,2},{6,4},{8,6},{10,8},{12,10},{14,12},{1,15},{3,1}... | collective-permute-start | bytes 393224 | tf_op jit(solution)/shard_map/ppermute | solution.py:188
  93.8 37.9 %copy-start = (s32[8,64]{1,0:T(8,128)S(1)}, s32[8,64]{1,0:T(8,128)}, u32[]{:S(2)}) copy-start(s32[8,64]{1,0:T(8,128)} %get-tuple-element.62.places_ref) | copy-start | bytes 6148
  93.9 5.8 %collective-permute-start.22 = (f16[128,512]{1,0:T(8,128)(2,1)S(1)}, f16[128,512]{1,0:T(8,128)(2,1)S(1)}, u32[]{:S(2)}, u32[]{:S(2)}) collective-permute-start(f16[128,512]{1,0:T(8,128)(2,1)S(1)} %get-tuple-element.109), channel_id=1, source_target_pairs={{0,14},{2,0},{4,2},{6,4},{8,6},{10,8},{12,10},{14,12},{1,15},{3,1}... | collective-permute-start | bytes 393224 | tf_op jit(solution)/shard_map/ppermute | solution.py:188
  96.4 7.9 %collective-permute-start.27 = (f16[128,512]{1,0:T(8,128)(2,1)S(1)}, f16[128,512]{1,0:T(8,128)(2,1)S(1)}, u32[]{:S(2)}, u32[]{:S(2)}) collective-permute-start(f16[128,512]{1,0:T(8,128)(2,1)S(1)} %get-tuple-element.117), channel_id=1, source_target_pairs={{0,2},{2,4},{4,6},{6,8},{8,10},{10,12},{12,14},{14,0},{1,3},{3,5},... | collective-permute-start | bytes 393224 | tf_op jit(solution)/shard_map/ppermute | solution.py:188
  96.6 7.7 %collective-permute-start.24 = (f16[128,512]{1,0:T(8,128)(2,1)S(1)}, f16[128,512]{1,0:T(8,128)(2,1)S(1)}, u32[]{:S(2)}, u32[]{:S(2)}) collective-permute-start(f16[128,512]{1,0:T(8,128)(2,1)S(1)} %add_convert_fusion.3), channel_id=1, source_target_pairs={{0,2},{2,4},{4,6},{6,8},{8,10},{10,12},{12,14},{14,0},{1,3},{3,5},... | collective-permute-start | bytes 393224 | tf_op jit(solution)/shard_map/ppermute | solution.py:188
  96.7 7.6 %collective-permute-start.29 = (f16[128,512]{1,0:T(8,128)(2,1)S(1)}, f16[128,512]{1,0:T(8,128)(2,1)S(1)}, u32[]{:S(2)}, u32[]{:S(2)}) collective-permute-start(f16[128,512]{1,0:T(8,128)(2,1)S(1)} %add_convert_fusion), channel_id=1, source_target_pairs={{0,14},{2,0},{4,2},{6,4},{8,6},{10,8},{12,10},{14,12},{1,15},{3,1}... | collective-permute-start | bytes 393224 | tf_op jit(solution)/shard_map/ppermute | solution.py:188
  106.4 12.5 %all-to-all-start.2 = ((f16[16,32,512]{2,1,0:T(8,128)(2,1)}), f16[16,32,512]{2,1,0:T(8,128)(2,1)S(1)}, u32[]{:S(2)}, u32[]{:S(2)}) async-start(f16[16,32,512]{2,1,0:T(8,128)(2,1)} %bitcast.5), calls=%async_computation.2 | async-start | bytes 1048576 | tf_op jit(solution)/shard_map/all_to_all | solution.py:323
  119.0 12.7 %collective-permute-start.30 = (f32[32,256]{1,0:T(8,128)S(1)}, f32[32,256]{1,0:T(8,128)S(1)}, u32[]{:S(2)}, u32[]{:S(2)}) collective-permute-start(f32[32,256]{1,0:T(8,128)S(1)} %get-tuple-element.119), channel_id=1, source_target_pairs={{0,1},{1,0},{2,3},{3,2},{4,5},{5,4},{6,7},{7,6},{8,9},{9,8},{10,11... | collective-permute-start | bytes 98312 | tf_op jit(solution)/shard_map/ppermute | solution.py:184
